TPU v7x, 32 devices: a whole 2x2x4 slice. The times are simulated.
32 devices in a mesh: layer: 4 (over y, x), feat: 8 (over z, core).
Axes of the slice: x: 2, y: 2, z: 4, core: 2. Of those that a mesh axis runs over, the one named last changes fastest.
Arguments:
- inputs: bfloat16 [4, 512, 2048], P('layer', 'feat'), may hold values from -6 to 6
- targets: bfloat16 [4, 512, 2048], P('layer', 'feat'), may hold values from -6 to 6
- enc_weight: bfloat16 [4, 2048, 16384], P('layer', None, 'feat'), may hold values from -0.125 to 0.125
- enc_bias: float32 [4, 16384], P('layer', 'feat'), may hold values from -1 to 0.5
- dec_weight: bfloat16 [4, 2, 16384, 2048], P('layer', None, 'feat'), may hold values from -0.046875 to 0.046875
- dec_bias: float32 [4, 2048], P('layer'), may hold values from -3 to 3
Outputs:
- mean_loss: float32 [], replicated
- enc_grad: bfloat16 [4, 2048, 16384], P('layer', None, 'feat')
- enc_bias_grad: float32 [4, 16384], P('layer', 'feat')
- dec_grad: bfloat16 [4, 2, 16384, 2048], P('layer', None, 'feat')
- dec_bias_grad: float32 [4, 2048], P('layer')
All inputs are finite; a program needn't handle non-finite values.
Results may differ from a plain program's by a relative error of at most 0.006.
Values may be sent and summed in bfloat16 or wider, within the bound.
No kernel may reach another device: no remote copies, remote signals or barrier semaphores. Data moves between devices by JAX's collectives and lax.ppermute only.
A program may use at most 128 MiB of HBM per device.

v0:
```python
import math

import jax
import jax.numpy as jnp
from jax import lax
from jax.experimental import pallas as pl
from jax.experimental.pallas import tpu as pltpu
from jax.sharding import PartitionSpec as P

f32, bf16 = jnp.float32, jnp.bfloat16
MIB = 2**20
VMEM = pl.BlockSpec(memory_space=pltpu.VMEM)
HBM = pl.BlockSpec(memory_space=pltpu.HBM)
ANY = pl.BlockSpec(memory_space=pl.ANY)


def swapped(block):
    size = lax.axis_size("feat")
    return lax.ppermute(block, "feat", [(i, i ^ 1) for i in range(size)])


def from_below(block, distance=1):
    size = lax.axis_size("feat")
    return lax.ppermute(block, "feat", [(i, (i + 2 * distance) % size) for i in range(size)])


def round_layers(block, distance):
    size = lax.axis_size("layer")
    return lax.ppermute(block, "layer", [(i, (i + distance) % size) for i in range(size)])


def after(value, *others):
    return lax.optimization_barrier((value, *others))[0]


def shape(dims, dtype):
    return jax.ShapeDtypeStruct(dims, dtype)


def call(name, kernel, flops, args, out_shape, limit, in_specs=None, out_specs=None, scratch=(), aliases=None):
    size = sum(math.prod(a.shape) * jnp.dtype(a.dtype).itemsize for a in (*args, *out_shape))
    return pl.pallas_call(
        kernel,
        in_specs=in_specs or [VMEM] * len(args),
        out_specs=out_specs or [VMEM] * len(out_shape),
        out_shape=out_shape,
        scratch_shapes=scratch,
        input_output_aliases=aliases or {},
        name=name,
        compiler_params=pltpu.CompilerParams(vmem_limit_bytes=limit * MIB),
        cost_estimate=pl.CostEstimate(flops=flops, bytes_accessed=size, transcendentals=0),
    )(*args)


def stacked(refs, at=slice(None)):
    return jnp.concatenate([ref[:, at] for ref in refs], axis=0)


def column_sums(values):
    return jnp.sum(values, axis=0, keepdims=True)


def over_tiles(size, body):
    tile = min(1024, size)

    @pl.loop(0, size // tile)
    def _(i):
        body(pl.ds(pl.multiple_of(i * tile, tile), tile))


def encode(token, weight_ref, bias_ref, pre_ref, act_ref):
    def body(at):
        pre = jnp.dot(token, weight_ref[:, at], preferred_element_type=f32) + bias_ref[:, at]
        pre = jnp.maximum(pre, 0.0)
        pre_ref[:, at] = pre
        act_ref[:, at] = (pre * pre).astype(bf16)

    over_tiles(weight_ref.shape[1], body)


def decode(act_ref, weight_refs, mine_ref, theirs_ref):
    rows = mine_ref.shape[0]
    width = weight_refs[0].shape[1]
    tile = min(1024, width)
    for k, weight_ref in enumerate(weight_refs):

        @pl.loop(0, width // tile)
        def _(i, k=k, weight_ref=weight_ref):
            at = pl.ds(pl.multiple_of(i * tile, tile), tile)
            to = pl.ds(pl.multiple_of(k * width + i * tile, tile), tile)
            out = jnp.dot(act_ref[...], weight_ref[:, at], preferred_element_type=f32)
            mine_ref[:, to] = out[:rows]
            theirs_ref[:, to] = out[rows:].astype(bf16)


def first_back(grad_refs, weight_ref, back_ref, sum_ref, square_ref):
    grad = stacked(grad_refs)
    wide = grad.astype(f32)
    sum_ref[...] += column_sums(wide)
    if square_ref is not None:
        square_ref[...] = column_sums(wide * wide)

    def body(at):
        back_ref[:, at] = jnp.dot(grad, weight_ref[:, at], preferred_element_type=f32)

    over_tiles(weight_ref.shape[1], body)


def second_back(grad_refs, weight_ref, back_ref, pre_ref, dpre_ref, sum_ref):
    grad = stacked(grad_refs)

    def body(at):
        out = back_ref[:, at] + jnp.dot(grad, weight_ref[:, at], preferred_element_type=f32)
        dpre = (out * 2.0 * pre_ref[:, at]).astype(bf16)
        dpre_ref[:, at] = dpre
        sum_ref[:, at] += column_sums(dpre.astype(f32))

    over_tiles(weight_ref.shape[1], body)


def outers(jobs, buffer_ref, sem_ref):
    copies = []
    for left_refs, right_refs, out_ref in jobs:
        rows, columns = out_ref.shape
        high, wide = min(1024, rows), min(512, columns)
        for start in range(0, rows, high):
            slot = len(copies) % 2
            if len(copies) >= 2:
                copies[-2].wait()
            turned = stacked(left_refs, pl.ds(start, high)).T
            for at in range(0, columns, wide):
                at = pl.ds(at, wide)
                out = jnp.dot(turned, stacked(right_refs, at), preferred_element_type=f32)
                buffer_ref[slot, :high, at] = out.astype(bf16)
            source = buffer_ref.at[slot, :high, :columns]
            copy = pltpu.make_async_copy(source, out_ref.at[pl.ds(start, high)], sem_ref.at[slot])
            copy.start()
            copies.append(copy)
    for copy in copies[-2:]:
        copy.wait()


def outer_scratch(rows, columns):
    return [pltpu.VMEM((2, min(1024, rows), columns), bf16), pltpu.SemaphoreType.DMA((2,))]


def prepared(tokens, encoder, decoders, bias):
    count = decoders.shape[0]
    rows, size = 2 * tokens[0].shape[0], encoder.shape[1]

    def kernel(mine_ref, theirs_ref, encoder_ref, decoders_ref, bias_ref, *refs):
        pre_ref, act_ref, weight_ref = refs[:3]
        mine, bias, sems = refs[-3:]
        sources = [mine_ref, bias_ref, encoder_ref] + [decoders_ref.at[k] for k in range(count)]
        targets = [mine, bias, *refs[2 : 3 + count]]
        copies = [
            pltpu.make_async_copy(source, target, sems.at[k])
            for k, (source, target) in enumerate(zip(sources, targets))
        ]
        for copy in copies:
            copy.start()
        for copy in copies[:3]:
            copy.wait()
        encode(stacked([mine, theirs_ref]), weight_ref, bias, pre_ref, act_ref)
        for copy in copies[3:]:
            copy.wait()

    out_shape = [shape((rows, size), f32), shape((rows, size), bf16)]
    out_shape += [pltpu.VMEM(encoder.shape, encoder.dtype)]
    out_shape += [pltpu.VMEM(decoders.shape[1:], decoders.dtype)] * count
    scratch = [pltpu.VMEM(tokens[0].shape, bf16), pltpu.VMEM(bias.shape, f32)]
    scratch.append(pltpu.SemaphoreType.DMA((3 + count,)))
    args = [tokens[0], encoder, decoders, bias]
    args = [pltpu.with_memory_space_constraint(array, pltpu.HBM) for array in args]
    args.insert(1, tokens[1])
    in_specs = [HBM, VMEM, HBM, HBM, HBM]
    return call("prepared", kernel, 2 * rows * encoder.size, args, out_shape, 8, in_specs, scratch=scratch)


def chunk(tokens, encoder, bias, decoders):
    rows, size = tokens[0].shape[0], encoder.shape[1]
    width = len(decoders) * decoders[0].shape[1]

    def kernel(mine_ref, theirs_ref, encoder_ref, bias_ref, *refs):
        pre_ref, act_ref, out_ref, other_ref = refs[len(decoders) :]
        encode(stacked([mine_ref, theirs_ref]), encoder_ref, bias_ref, pre_ref, act_ref)
        decode(act_ref, refs[: len(decoders)], out_ref, other_ref)

    out_shape = [shape((2 * rows, size), f32), shape((2 * rows, size), bf16)]
    out_shape += [shape((rows, width), f32), shape((rows, width), bf16)]
    flops = 4 * rows * (encoder.size + len(decoders) * decoders[0].size)
    return call("chunk", kernel, flops, [*tokens, encoder, bias, *decoders], out_shape, 8)


def decoded(act, decoders):
    rows, width = act.shape[0] // 2, len(decoders) * decoders[0].shape[1]

    def kernel(act_ref, *refs):
        decode(act_ref, refs[: len(decoders)], *refs[len(decoders) :])

    out_shape = [shape((rows, width), f32), shape((rows, width), bf16)]
    flops = 4 * rows * len(decoders) * decoders[0].size
    return call("decoded", kernel, flops, [act, *decoders], out_shape, 8)


def transposed(weight):
    rows, columns = weight.shape
    tile = min(256, rows)

    def kernel(weight_ref, out_ref):
        @pl.loop(0, rows // tile)
        def _(i):
            at = pl.ds(pl.multiple_of(i * tile, tile), tile)
            out_ref[:, at] = weight_ref[at, :].T

    out_shape = [pltpu.VMEM((columns, rows), weight.dtype)]
    return call("transposed", kernel, 256 * rows * columns, [weight], out_shape, 4)[0]


def backward(weights, firsts, seconds, sums, jobs=(), held=None):
    width, size = weights[0].shape
    args, places = [], {}

    def add(array):
        if id(array) not in places:
            places[id(array)] = len(args)
            args.append(array)
        return places[id(array)]

    def add_all(arrays):
        return [array if isinstance(array, int) else (add(array),) for array in arrays]

    weight_at = [add(weight) for weight in weights]
    first_at = [add_all(pair) for pair in firsts]
    second_at = [(add_all(pair), add(back), add(pre)) for pair, back, pre in seconds]
    job_at = [(add_all(left), add_all(right)) for left, right, _, _ in jobs]
    sums_at = [add(array) for array in sums]
    count, backs, dpres = len(args) + (held is not None), len(firsts), len(seconds)

    def kernel(*refs):
        ins, outs = refs[:count], refs[count:]
        dpre_refs = outs[backs : backs + dpres]
        grad_sum_ref, dpre_sum_ref = outs[backs + dpres : backs + dpres + 2]
        job_refs, scratch = outs[backs + dpres + 2 :][: len(jobs)], outs[backs + dpres + 2 + len(jobs) :]

        def pick(ats):
            return [dpre_refs[at] if isinstance(at, int) else ins[at[0]] for at in ats]

        for k, sum_ref in enumerate((grad_sum_ref, dpre_sum_ref)):
            sum_ref[...] = ins[sums_at[k]][...] if sums else jnp.zeros(sum_ref.shape, f32)
        square_ref = None if sums else outs[backs + dpres + 2]
        for at, back_ref in zip(first_at, outs):
            first_back(pick(at), ins[weight_at[0]], back_ref, grad_sum_ref, square_ref)
        for (at, back, pre), dpre_ref in zip(second_at, dpre_refs):
            second_back(pick(at), ins[weight_at[1]], ins[back], ins[pre], dpre_ref, dpre_sum_ref)
        work = [
            (pick(left), pick(right), out_ref.at[index])
            for (left, right), out_ref, (_, _, _, index) in zip(job_at, job_refs, jobs)
        ]
        if work:
            outers(work, *scratch)

    out_shape = [shape((2 * pair[0].shape[0], size), f32) for pair in firsts]
    out_shape += [shape(pre.shape, bf16) for _, _, pre in seconds]
    out_shape += [shape((1, width), f32), shape((1, size), f32)] + [shape((1, width), f32)] * (not sums)
    in_specs, out_specs = [VMEM] * len(args), [VMEM] * len(out_shape)
    flops = 2 * sum(part.size for part in out_shape[: backs + dpres]) * width
    scratch, aliases = [], {}
    for left, right, lead, _ in jobs:
        columns = size if isinstance(right[-1], int) else right[0].shape[1]
        out_shape.append(shape((lead, left[0].shape[1], columns), bf16))
        out_specs.append(ANY)
        flops += 2 * out_shape[-1].size // lead * sum(part.shape[0] for part in left)
    if jobs:
        scratch = outer_scratch(max(size, width), max(part.shape[2] for part in out_shape[-len(jobs) :]))
    if held is not None:
        aliases = {len(args): backs + dpres + 2}
        args.append(held)
        in_specs.append(ANY)
    limit = 16 if jobs else 6
    outs = call("backward", kernel, flops, args, out_shape, limit, in_specs, out_specs, scratch, aliases)
    return outs[:backs], outs[backs : backs + dpres], outs[backs + dpres :]


def shards(inputs, targets, enc_weight, enc_bias, dec_weight, dec_bias):
    rows = inputs.shape[1]
    width = dec_weight.shape[3]
    layers, chips = lax.axis_size("layer"), lax.axis_size("feat") // 2
    layer = jnp.zeros((width,), f32) + lax.axis_index("layer").astype(f32)
    held, layer = lax.optimization_barrier((inputs[0], layer))
    inner, final = layer > 0.0, layer == layers - 1.0

    tokens = [(held, swapped(held))]
    pre, act, encoder, *decoders = prepared(tokens[0], enc_weight[0], dec_weight[0], enc_bias)
    pres, acts, sums = [pre], [act], [None] * chips

    def spread(j, mine, theirs):
        both = mine + swapped(theirs).astype(f32)
        later = both[:, width:].astype(bf16)
        sums[j] = both[:, :width], round_layers(later, 1)
        return later

    def run(j, *others):
        held, other = tokens[j]
        pre, act, mine, theirs = chunk((after(held, *others), other), encoder, enc_bias, decoders)
        pres.append(pre)
        acts.append(act)
        return mine, theirs

    def summed(j):
        here, later = sums[j]
        return here + jnp.where(inner, later.astype(f32), 0.0)

    order = list(range(1, chips)) + [0]
    total, done = None, acts[0]
    if chips > 1:
        held = after(from_below(tokens[0][0]), done)
        tokens.append((held, swapped(held)))
    for j in order:
        if j == 0:
            break
        mine, theirs = run(j, *([total] if j > 2 else [done]))
        if j == 1:
            first = decoded(after(acts[0], theirs), decoders)
            done = first[1]
        if j < chips - 1:
            theirs, held, done = lax.optimization_barrier((theirs, from_below(tokens[-1][0]), done))
            tokens.append((held, swapped(held)))
        if j == 2:
            total = summed(1)
        if j > 2:
            arrived = from_below(total.astype(bf16)).astype(f32)
            total = arrived + summed(j - 1)
            theirs = after(theirs, total)
        done = spread(j, mine, theirs)
        if j == 1:
            spread(0, *first)
    if chips < 3:
        total = summed(order[0])
    decoders_t = []
    for j in order[max(chips - 2, 1) :]:
        arrived = from_below(total.astype(bf16))
        if len(decoders_t) < len(decoders):
            decoders_t.append(transposed(after(decoders[len(decoders_t)], total)))
            arrived = after(arrived, decoders_t[-1])
        total = arrived.astype(f32) + summed(j)
    decoders_t += [transposed(decoder) for decoder in decoders[len(decoders_t) :]]

    grad = (total + dec_bias[0] - targets[0].astype(f32)).astype(bf16)

    here, later, backs, dpres, acc = [(grad, swapped(grad))], [], [], [], []
    (back,), _, (*acc, squares) = backward(decoders_t, here, [], [])
    done, dec_grad, pending = back, None, []
    entries = layers * lax.axis_size("feat") * rows * width
    hops = [[(from_below, k) for k in range(1, chips)], [(round_layers, k) for k in range(1, layers)]]
    for j in range(chips):
        if j < chips - 1:
            held = done = after(from_below(here[j][0]), done)
        ahead = after(round_layers(here[j][0], -1), done)
        ahead = jnp.where(final, jnp.zeros_like(ahead), ahead)
        if pending:
            squares = sum(after(block, ahead) for block in pending) + squares
            held, ahead = lax.optimization_barrier((held, ahead, squares))[:2]
        if j < chips - 1:
            here.append((held, swapped(held)))
        later.append((ahead, swapped(ahead)))
        pending = []
        if hops and j < chips - 1:
            pending = [move(squares, distance) for move, distance in hops.pop(0)]
        if j == chips - 1:
            break
        jobs = []
        if j == chips - 2:
            jobs = [(acts, [part for pair in here for part in pair], 2, 0)]
        (back,), (dpre,), acc = backward(
            decoders_t, [here[j + 1]], [(later[j], back, pres[j])], acc[:2], jobs
        )
        dpres.append(dpre)
        done, dec_grad = dpre, acc[-1]

    flat = [part for pair in tokens for part in pair]
    jobs = [(acts, [part for pair in later for part in pair], 2, 1), (flat, [*dpres, 0], 1, 0)]
    _, _, (grad_sum, dpre_sum, dec_grad, enc_grad) = backward(
        decoders_t, [], [(later[-1], back, pres[-1])], acc[:2], jobs, dec_grad
    )
    for moves in hops:
        squares = sum(move(squares, distance) for move, distance in moves) + squares
    return (jnp.sum(squares / entries), enc_grad, dpre_sum, dec_grad[None], grad_sum)


def solution(mesh):
    return jax.shard_map(
        shards,
        mesh=mesh,
        in_specs=(
            P("layer", "feat", None),
            P("layer", "feat", None),
            P("layer", None, "feat"),
            P("layer", "feat"),
            P("layer", None, "feat", None),
            P("layer", None),
        ),
        out_specs=(
            P(),
            P("layer", None, "feat"),
            P("layer", "feat"),
            P("layer", None, "feat", None),
            P("layer", None),
        ),
        check_vma=False,
    )
```

profile of v0, /device:TPU:0, one launch (start us, length us, event | category | flops | bytes accessed | tf_op | source)
XLA Modules:
  0.0 127.6 jit_solution(9897506685698399568)
XLA Ops:
  0.6 0.5 collective-permute-start
  1.2 2.6 %collective-permute-start.1 = (bf16[64,2048]{1,0:T(8,128)(2,1)}, bf16[64,2048]{1,0:T(8,128)(2,1)S(1)}, u32[]{:S(2)}, u32[]{:S(2)}) collective-permute-start(bf16[64,2048]{1,0:T(8,128)(2,1)} %bitcast.11), channel_id=1, source_target_pairs={{0,2},{1,3},{2,4},{3,5},{4,6},{5,7},{6,0},{7,1},{8,10},{9,11},{10,... | collective-permute-start | bytes 786440 | tf_op jit(solution)/shard_map/ppermute | solution.py:24
  3.8 8.3 %prepared.1 = (f32[128,2048]{1,0:T(8,128)S(1)}, bf16[128,2048]{1,0:T(8,128)(2,1)S(1)}, bf16[2048,2048]{1,0:T(8,128)(2,1)S(1)}, bf16[2048,2048]{1,0:T(8,128)(2,1)S(1)}, bf16[2048,2048]{1,0:T(8,128)(2,1)S(1)}) custom-call(bf16[64,2048]{1,0:T(8,128)(2,1)} %bitcast.12, bf16[64,2048]{1,0:T(8,128)(2,1)S(1)} %collective-permute-done.theirs_ref.refs_17_, ...), custom_call_target="tpu_custom_call" | custom-call | flops 1073741824 | bytes 52436992 | tf_op jit(solution)/shard_map/prepared/pallas_call | solution.py:42
  12.2 0.8 collective-permute-done.1.mine_ref.refs_18_
  13.0 1.1 collective-permute-start.3
  14.1 0.4 collective-permute-done.2.theirs_ref.refs_19_
  14.5 4.5 %chunk.3 = (f32[128,2048]{1,0:T(8,128)S(1)}, bf16[128,2048]{1,0:T(8,128)(2,1)S(1)}, f32[64,4096]{1,0:T(8,128)S(1)}, bf16[64,4096]{1,0:T(8,128)(2,1)S(1)}) custom-call(bf16[64,2048]{1,0:T(8,128)(2,1)S(1)} %collective-permute-done.1.mine_ref.refs_18_, bf16[64,2048]{1,0:T(8,128)(2,1)S(1)} %collective-permute-done.2.theirs_ref.refs_19_, ...), custom_call_target="tpu_custom_call" | custom-call | flops 3221225472 | bytes 28844032 | tf_op jit(solution)/shard_map/chunk/pallas_call | solution.py:42
  19.0 2.9 %decoded.1 = (f32[64,4096]{1,0:T(8,128)S(1)}, bf16[64,4096]{1,0:T(8,128)(2,1)S(1)}) custom-call(bf16[128,2048]{1,0:T(8,128)(2,1)S(1)} %get-tuple-element.87.act_ref.refs_8_.refs_6_, bf16[2048,2048]{1,0:T(8,128)(2,1)S(1)} %get-tuple-element.96.refs_0_.weight_ref, bf16[2048,2048]{1,0:T(8,128)(2,1)S(1)} %get-tuple-element.103.refs_1_.weight_ref), custom_call_target="tpu_custom_call" | custom-call | flops 2147483648 | bytes 18874368 | tf_op jit(solution)/shard_map/decoded/pallas_call | solution.py:42
  22.0 1.5 %collective-permute-done.3.mine_ref.refs_20_ = bf16[64,2048]{1,0:T(8,128)(2,1)S(1)} collective-permute-done((bf16[64,2048]{1,0:T(8,128)(2,1)S(1)}, bf16[64,2048]{1,0:T(8,128)(2,1)S(1)}, u32[]{:S(2)}, u32[]{:S(2)}) %collective-permute-start.3) | collective-permute-done | bytes 262176 | tf_op jit(solution)/shard_map/ppermute | solution.py:24
  23.5 0.5 collective-permute-start.7
  24.0 1.4 %collective-permute-done.4 = bf16[64,4096]{1,0:T(8,128)(2,1)S(1)} collective-permute-done((bf16[64,4096]{1,0:T(8,128)(2,1)S(1)}, bf16[64,4096]{1,0:T(8,128)(2,1)S(1)}, u32[]{:S(2)}, u32[]{:S(2)}) %collective-permute-start.4) | collective-permute-done | bytes 524320 | tf_op jit(solution)/shard_map/ppermute | solution.py:19
  25.4 0.1 convert_add_fusion.3
  25.5 1.5 %collective-permute-start.5 = (bf16[64,2048]{1,0:T(8,128)(2,1)S(1)}, bf16[64,2048]{1,0:T(8,128)(2,1)S(1)}, u32[]{:S(2)}, u32[]{:S(2)}) collective-permute-start(bf16[64,2048]{1,0:T(8,128)(2,1)S(1)} %slice.67), channel_id=1, source_target_pairs={{0,8},{8,16},{16,24},{24,0},{1,9},{9,17},{17,25},{25,1},{2,10},{10... | collective-permute-start | bytes 786440 | tf_op jit(solution)/shard_map/ppermute | solution.py:29
  27.1 4.5 %chunk.4 = (f32[128,2048]{1,0:T(8,128)S(1)}, bf16[128,2048]{1,0:T(8,128)(2,1)S(1)}, f32[64,4096]{1,0:T(8,128)S(1)}, bf16[64,4096]{1,0:T(8,128)(2,1)S(1)}) custom-call(bf16[64,2048]{1,0:T(8,128)(2,1)S(1)} %collective-permute-done.3.mine_ref.refs_20_, bf16[64,2048]{1,0:T(8,128)(2,1)S(1)} %collective-permute-done.7.theirs_ref.refs_21_, ...), custom_call_target="tpu_custom_call" | custom-call | flops 3221225472 | bytes 28844032 | tf_op jit(solution)/shard_map/chunk/pallas_call | solution.py:42
  31.6 2.4 %collective-permute-done.8.mine_ref.refs_22_ = bf16[64,2048]{1,0:T(8,128)(2,1)S(1)} collective-permute-done((bf16[64,2048]{1,0:T(8,128)(2,1)S(1)}, bf16[64,2048]{1,0:T(8,128)(2,1)S(1)}, u32[]{:S(2)}, u32[]{:S(2)}) %collective-permute-start.8) | collective-permute-done | bytes 262176 | tf_op jit(solution)/shard_map/ppermute | solution.py:24
  34.0 0.5 collective-permute-start.12
  34.5 0.3 collective-permute-done.5
  35.0 0.9 collective-permute-done.9
  35.9 0.1 convert_add_fusion.2
  36.0 1.5 %collective-permute-start.10 = (bf16[64,2048]{1,0:T(8,128)(2,1)S(1)}, bf16[64,2048]{1,0:T(8,128)(2,1)S(1)}, u32[]{:S(2)}, u32[]{:S(2)}) collective-permute-start(bf16[64,2048]{1,0:T(8,128)(2,1)S(1)} %slice.66), channel_id=1, source_target_pairs={{0,8},{8,16},{16,24},{24,0},{1,9},{9,17},{17,25},{25,1},{2,10},{10... | collective-permute-start | bytes 786440 | tf_op jit(solution)/shard_map/ppermute | solution.py:29
  37.6 4.5 %chunk.5 = (f32[128,2048]{1,0:T(8,128)S(1)}, bf16[128,2048]{1,0:T(8,128)(2,1)S(1)}, f32[64,4096]{1,0:T(8,128)S(1)}, bf16[64,4096]{1,0:T(8,128)(2,1)S(1)}) custom-call(bf16[64,2048]{1,0:T(8,128)(2,1)S(1)} %collective-permute-done.8.mine_ref.refs_22_, bf16[64,2048]{1,0:T(8,128)(2,1)S(1)} %collective-permute-done.12.theirs_ref.refs_23_, ...), custom_call_target="tpu_custom_call" | custom-call | flops 3221225472 | bytes 28844032 | tf_op jit(solution)/shard_map/chunk/pallas_call | solution.py:42
  42.1 2.6 %collective-permute-done.6 = bf16[64,2048]{1,0:T(8,128)(2,1)S(1)} collective-permute-done((bf16[64,2048]{1,0:T(8,128)(2,1)S(1)}, bf16[64,2048]{1,0:T(8,128)(2,1)S(1)}, u32[]{:S(2)}, u32[]{:S(2)}) %collective-permute-start.6) | collective-permute-done | bytes 262176 | tf_op jit(solution)/shard_map/ppermute | solution.py:24
  44.7 0.6 collective-permute-done.10
  45.3 0.1 fusion.5
  45.4 0.1 collective-permute-start.13
  45.6 1.8 %collective-permute-done.13 = bf16[64,4096]{1,0:T(8,128)(2,1)S(1)} collective-permute-done((bf16[64,4096]{1,0:T(8,128)(2,1)S(1)}, bf16[64,4096]{1,0:T(8,128)(2,1)S(1)}, u32[]{:S(2)}, u32[]{:S(2)}) %collective-permute-start.13) | collective-permute-done | bytes 524320 | tf_op jit(solution)/shard_map/ppermute | solution.py:19
  47.4 0.1 convert_add_fusion.1
  47.6 0.9 collective-permute-start.14
  48.5 2.8 %transposed.2.refs_0_ = bf16[2048,2048]{1,0:T(8,128)(2,1)S(1)} custom-call(bf16[2048,2048]{1,0:T(8,128)(2,1)S(1)} %get-tuple-element.96.refs_0_.weight_ref), custom_call_target="tpu_custom_call" | custom-call | flops 1073741824 | bytes 16777216 | tf_op jit(solution)/shard_map/transposed/pallas_call | solution.py:42
  51.3 4.7 %collective-permute-done.11 = bf16[64,2048]{1,0:T(8,128)(2,1)S(1)} collective-permute-done((bf16[64,2048]{1,0:T(8,128)(2,1)S(1)}, bf16[64,2048]{1,0:T(8,128)(2,1)S(1)}, u32[]{:S(2)}, u32[]{:S(2)}) %collective-permute-start.11) | collective-permute-done | bytes 262176 | tf_op jit(solution)/shard_map/ppermute | solution.py:24
  56.0 0.9 collective-permute-done.14
  56.9 0.1 fusion.4
  57.1 0.1 convert_add_fusion
  57.3 2.8 %transposed.3.refs_1_ = bf16[2048,2048]{1,0:T(8,128)(2,1)S(1)} custom-call(bf16[2048,2048]{1,0:T(8,128)(2,1)S(1)} %bitcast.9), custom_call_target="tpu_custom_call" | custom-call | flops 1073741824 | bytes 16777216 | tf_op jit(solution)/shard_map/transposed/pallas_call | solution.py:42
  60.2 6.2 %collective-permute-done.15 = bf16[64,2048]{1,0:T(8,128)(2,1)S(1)} collective-permute-done((bf16[64,2048]{1,0:T(8,128)(2,1)S(1)}, bf16[64,2048]{1,0:T(8,128)(2,1)S(1)}, u32[]{:S(2)}, u32[]{:S(2)}) %collective-permute-start.15) | collective-permute-done | bytes 262176 | tf_op jit(solution)/shard_map/ppermute | solution.py:24
  66.4 0.2 fusion.3.refs_2_.refs_12_
  66.6 0.1 collective-permute-start.18
  66.6 0.6 collective-permute-start.20
  67.3 1.0 collective-permute-start.24
  68.3 1.7 %backward.5 = (f32[128,2048]{1,0:T(8,128)S(1)}, f32[1,2048]{1,0:T(1,128)S(1)}, f32[1,2048]{1,0:T(1,128)S(1)}, f32[1,2048]{1,0:T(1,128)S(1)}) custom-call(bf16[2048,2048]{1,0:T(8,128)(2,1)S(1)} %transposed.2.refs_0_, bf16[2048,2048]{1,0:T(8,128)(2,1)S(1)} %transposed.3.refs_1_, bf16[64,2048]{1,0:T(8,128)(2,1)S(1)} %fusion.3.refs_2_.refs_12_, ...), custom_call_target="tpu_custom_call" | custom-call | flops 1073741824 | bytes 18374656 | tf_op jit(solution)/shard_map/backward/pallas_call | solution.py:42
  70.0 7.2 %collective-permute-done.20.refs_2_.refs_14_ = bf16[64,2048]{1,0:T(8,128)(2,1)S(1)} collective-permute-done((bf16[64,2048]{1,0:T(8,128)(2,1)S(1)}, bf16[64,2048]{1,0:T(8,128)(2,1)S(1)}, u32[]{:S(2)}, u32[]{:S(2)}) %collective-permute-start.20) | collective-permute-done | bytes 262176 | tf_op jit(solution)/shard_map/ppermute | solution.py:24
  77.3 0.5 collective-permute-start.23
  77.8 0.3 collective-permute-start.22
  78.0 1.2 collective-permute-start.21
  79.3 3.6 %collective-permute-start.27 = (f32[1,2048]{1,0:T(1,128)S(1)}, f32[1,2048]{1,0:T(1,128)S(1)}, u32[]{:S(2)}, u32[]{:S(2)}) collective-permute-start(f32[1,2048]{1,0:T(1,128)S(1)} %get-tuple-element.106), channel_id=1, source_target_pairs={{0,6},{1,7},{2,0},{3,1},{4,2},{5,3},{6,4},{7,5},{8,14},{9,15},{10,... | collective-permute-start | bytes 24584 | tf_op jit(solution)/shard_map/ppermute | solution.py:24
  82.9 1.4 %collective-permute-start.19 = (f32[1,2048]{1,0:T(1,128)S(1)}, f32[1,2048]{1,0:T(1,128)S(1)}, u32[]{:S(2)}, u32[]{:S(2)}) collective-permute-start(f32[1,2048]{1,0:T(1,128)S(1)} %get-tuple-element.106), channel_id=1, source_target_pairs={{0,2},{1,3},{2,4},{3,5},{4,6},{5,7},{6,0},{7,1},{8,10},{9,11},{10,... | collective-permute-start | bytes 24584 | tf_op jit(solution)/shard_map/ppermute | solution.py:24
  84.3 3.1 %backward.6 = (f32[128,2048]{1,0:T(8,128)S(1)}, bf16[128,2048]{1,0:T(8,128)(2,1)S(1)}, f32[1,2048]{1,0:T(1,128)S(1)}, f32[1,2048]{1,0:T(1,128)S(1)}) custom-call(bf16[2048,2048]{1,0:T(8,128)(2,1)S(1)} %transposed.2.refs_0_, bf16[2048,2048]{1,0:T(8,128)(2,1)S(1)} %transposed.3.refs_1_, bf16[64,2048]{1,0:T(8,128)(2,1)S(1)} %collective-permute-done.20.refs_2_.refs_14_, ...), custom_call_target="tpu_custom_call" | custom-call | flops 2147483648 | bytes 21528576 | tf_op jit(solution)/shard_map/backward/pallas_call | solution.py:42
  87.5 0.7 collective-permute-done.22.refs_2_.refs_16_
  88.2 0.4 collective-permute-done.26
  88.6 0.1 collective-permute-start.32
  88.7 0.5 collective-permute-start.31
  89.1 1.1 collective-permute-start.30
  90.2 1.7 %collective-permute-start.29 = (bf16[64,2048]{1,0:T(8,128)(2,1)S(1)}, bf16[64,2048]{1,0:T(8,128)(2,1)S(1)}, u32[]{:S(2)}, u32[]{:S(2)}) collective-permute-start(bf16[64,2048]{1,0:T(8,128)(2,1)S(1)} %collective-permute-done.22.refs_2_.refs_16_), channel_id=1, source_target_pairs={{0,24},{8,0},{16,8},{24,16},{1,25},{9,1},{17,9},{25,17},{2,26},{10... | collective-permute-start | bytes 786440 | tf_op jit(solution)/shard_map/ppermute | solution.py:29
  91.9 0.7 collective-permute-start.34
  92.6 1.1 collective-permute-start.33
  93.7 0.7 collective-permute-start.28
  94.4 3.2 %backward.7 = (f32[128,2048]{1,0:T(8,128)S(1)}, bf16[128,2048]{1,0:T(8,128)(2,1)S(1)}, f32[1,2048]{1,0:T(1,128)S(1)}, f32[1,2048]{1,0:T(1,128)S(1)}) custom-call(bf16[2048,2048]{1,0:T(8,128)(2,1)S(1)} %transposed.2.refs_0_, bf16[2048,2048]{1,0:T(8,128)(2,1)S(1)} %transposed.3.refs_1_, bf16[64,2048]{1,0:T(8,128)(2,1)S(1)} %collective-permute-done.22.refs_2_.refs_16_, ...), custom_call_target="tpu_custom_call" | custom-call | flops 2147483648 | bytes 21528576 | tf_op jit(solution)/shard_map/backward/pallas_call | solution.py:42
  97.6 1.6 %collective-permute-done.30.refs_2_ = bf16[64,2048]{1,0:T(8,128)(2,1)S(1)} collective-permute-done((bf16[64,2048]{1,0:T(8,128)(2,1)S(1)}, bf16[64,2048]{1,0:T(8,128)(2,1)S(1)}, u32[]{:S(2)}, u32[]{:S(2)}) %collective-permute-start.30) | collective-permute-done | bytes 262176 | tf_op jit(solution)/shard_map/ppermute | solution.py:24
  99.3 0.6 multiply_reduce_fusion
  99.9 0.5 collective-permute-start.37
  100.4 1.9 %collective-permute-start.35 = (bf16[64,2048]{1,0:T(8,128)(2,1)S(1)}, bf16[64,2048]{1,0:T(8,128)(2,1)S(1)}, u32[]{:S(2)}, u32[]{:S(2)}) collective-permute-start(bf16[64,2048]{1,0:T(8,128)(2,1)S(1)} %collective-permute-done.30.refs_2_), channel_id=1, source_target_pairs={{0,24},{8,0},{16,8},{24,16},{1,25},{9,1},{17,9},{25,17},{2,26},{10... | collective-permute-start | bytes 786440 | tf_op jit(solution)/shard_map/ppermute | solution.py:29
  102.3 9.7 %backward.8 = (f32[128,2048]{1,0:T(8,128)S(1)}, bf16[128,2048]{1,0:T(8,128)(2,1)S(1)}, f32[1,2048]{1,0:T(1,128)S(1)}, f32[1,2048]{1,0:T(1,128)S(1)}, bf16[2,2048,2048]{2,1,0:T(8,128)(2,1)}) custom-call(bf16[2048,2048]{1,0:T(8,128)(2,1)S(1)} %transposed.2.refs_0_, bf16[2048,2048]{1,0:T(8,128)(2,1)S(1)} %transposed.3.refs_1_, ...), custom_call_target="tpu_custom_call" | custom-call | flops 6442450944 | bytes 41975808 | tf_op jit(solution)/shard_map/backward/pallas_call | solution.py:42
  112.2 1.5 %collective-permute-done.38.refs_3_ = bf16[64,2048]{1,0:T(8,128)(2,1)S(1)} collective-permute-done((bf16[64,2048]{1,0:T(8,128)(2,1)S(1)}, bf16[64,2048]{1,0:T(8,128)(2,1)S(1)}, u32[]{:S(2)}, u32[]{:S(2)}) %collective-permute-start.38) | collective-permute-done | bytes 262176 | tf_op jit(solution)/shard_map/ppermute | solution.py:19
  113.7 13.7 %backward.9 = (bf16[128,2048]{1,0:T(8,128)(2,1)}, f32[1,2048]{1,0:T(1,128)}, f32[1,2048]{1,0:T(1,128)}, bf16[2,2048,2048]{2,1,0:T(8,128)(2,1)}, bf16[1,2048,2048]{2,1,0:T(8,128)(2,1)}) custom-call(bf16[2048,2048]{1,0:T(8,128)(2,1)S(1)} %transposed.2.refs_0_, bf16[2048,2048]{1,0:T(8,128)(2,1)S(1)} %transposed.3.refs_1_, ...), custom_call_target="tpu_custom_call", output_to_operand_aliasing={{3}: (29, {})} | custom-call | flops 9663676416 | bytes 69238784 | tf_op jit(solution)/shard_map/backward/pallas_call | solution.py:42
  (61 shorter events, 0.8 us)
Async XLA Ops:
  0.6 3.2 %collective-permute-start = (bf16[64,2048]{1,0:T(8,128)(2,1)}, bf16[64,2048]{1,0:T(8,128)(2,1)S(1)}, u32[]{:S(2)}, u32[]{:S(2)}) collective-permute-start(bf16[64,2048]{1,0:T(8,128)(2,1)} %bitcast.10), channel_id=1, source_target_pairs={{0,1},{1,0},{2,3},{3,2},{4,5},{5,4},{6,7},{7,6},{8,9},{9,8},{10,11... | collective-permute-start | bytes 786440 | tf_op jit(solution)/shard_map/ppermute | solution.py:19
  1.2 11.8 %collective-permute-start.1 = (bf16[64,2048]{1,0:T(8,128)(2,1)}, bf16[64,2048]{1,0:T(8,128)(2,1)S(1)}, u32[]{:S(2)}, u32[]{:S(2)}) collective-permute-start(bf16[64,2048]{1,0:T(8,128)(2,1)} %bitcast.11), channel_id=1, source_target_pairs={{0,2},{1,3},{2,4},{3,5},{4,6},{5,7},{6,0},{7,1},{8,10},{9,11},{10,... | collective-permute-start | bytes 786440 | tf_op jit(solution)/shard_map/ppermute | solution.py:24
  3.8 10.7 %copy-start.2 = (f32[1,2048]{1,0:T(1,128)S(1)}, f32[1,2048]{1,0:T(1,128)}, u32[]{:S(2)}) copy-start(f32[1,2048]{1,0:T(1,128)} %bias_ref.7) | copy-start | bytes 24580
  12.1 25.4 %copy-start = (bf16[2048,2048]{1,0:T(8,128)(2,1)}, bf16[2048,2048]{1,0:T(8,128)(2,1)S(1)}, u32[]{:S(2)}) copy-start(bf16[2048,2048]{1,0:T(8,128)(2,1)S(1)} %get-tuple-element.103.refs_1_.weight_ref) | copy-start | bytes 25165828
  12.9 1.5 %collective-permute-start.2 = (bf16[64,2048]{1,0:T(8,128)(2,1)S(1)}, bf16[64,2048]{1,0:T(8,128)(2,1)S(1)}, u32[]{:S(2)}, u32[]{:S(2)}) collective-permute-start(bf16[64,2048]{1,0:T(8,128)(2,1)S(1)} %collective-permute-done.1.mine_ref.refs_18_), channel_id=1, source_target_pairs={{0,1},{1,0},{2,3},{3,2},{4,5},{5,4},{6,7},{7,6},{8,9},{9,8},{10,11... | collective-permute-start | bytes 786440 | tf_op jit(solution)/shard_map/ppermute | solution.py:19
  13.0 10.5 %collective-permute-start.3 = (bf16[64,2048]{1,0:T(8,128)(2,1)S(1)}, bf16[64,2048]{1,0:T(8,128)(2,1)S(1)}, u32[]{:S(2)}, u32[]{:S(2)}) collective-permute-start(bf16[64,2048]{1,0:T(8,128)(2,1)S(1)} %collective-permute-done.1.mine_ref.refs_18_), channel_id=1, source_target_pairs={{0,2},{1,3},{2,4},{3,5},{4,6},{5,7},{6,0},{7,1},{8,10},{9,11},{10,... | collective-permute-start | bytes 786440 | tf_op jit(solution)/shard_map/ppermute | solution.py:24
  23.5 1.9 %collective-permute-start.4 = (bf16[64,4096]{1,0:T(8,128)(2,1)S(1)}, bf16[64,4096]{1,0:T(8,128)(2,1)S(1)}, u32[]{:S(2)}, u32[]{:S(2)}) collective-permute-start(bf16[64,4096]{1,0:T(8,128)(2,1)S(1)} %get-tuple-element.89), channel_id=1, source_target_pairs={{0,1},{1,0},{2,3},{3,2},{4,5},{5,4},{6,7},{7,6},{8,9},{9,8},{10,11... | collective-permute-start | bytes 1572872 | tf_op jit(solution)/shard_map/ppermute | solution.py:19
  23.5 10.5 %collective-permute-start.8 = (bf16[64,2048]{1,0:T(8,128)(2,1)S(1)}, bf16[64,2048]{1,0:T(8,128)(2,1)S(1)}, u32[]{:S(2)}, u32[]{:S(2)}) collective-permute-start(bf16[64,2048]{1,0:T(8,128)(2,1)S(1)} %collective-permute-done.3.mine_ref.refs_20_), channel_id=1, source_target_pairs={{0,2},{1,3},{2,4},{3,5},{4,6},{5,7},{6,0},{7,1},{8,10},{9,11},{10,... | collective-permute-start | bytes 786440 | tf_op jit(solution)/shard_map/ppermute | solution.py:24
  23.5 3.6 %collective-permute-start.7 = (bf16[64,2048]{1,0:T(8,128)(2,1)S(1)}, bf16[64,2048]{1,0:T(8,128)(2,1)S(1)}, u32[]{:S(2)}, u32[]{:S(2)}) collective-permute-start(bf16[64,2048]{1,0:T(8,128)(2,1)S(1)} %collective-permute-done.3.mine_ref.refs_20_), channel_id=1, source_target_pairs={{0,1},{1,0},{2,3},{3,2},{4,5},{5,4},{6,7},{7,6},{8,9},{9,8},{10,11... | collective-permute-start | bytes 786440 | tf_op jit(solution)/shard_map/ppermute | solution.py:19
  25.5 9.3 %collective-permute-start.5 = (bf16[64,2048]{1,0:T(8,128)(2,1)S(1)}, bf16[64,2048]{1,0:T(8,128)(2,1)S(1)}, u32[]{:S(2)}, u32[]{:S(2)}) collective-permute-start(bf16[64,2048]{1,0:T(8,128)(2,1)S(1)} %slice.67), channel_id=1, source_target_pairs={{0,8},{8,16},{16,24},{24,0},{1,9},{9,17},{17,25},{25,1},{2,10},{10... | collective-permute-start | bytes 786440 | tf_op jit(solution)/shard_map/ppermute | solution.py:29
  34.0 1.9 %collective-permute-start.9 = (bf16[64,4096]{1,0:T(8,128)(2,1)S(1)}, bf16[64,4096]{1,0:T(8,128)(2,1)S(1)}, u32[]{:S(2)}, u32[]{:S(2)}) collective-permute-start(bf16[64,4096]{1,0:T(8,128)(2,1)S(1)} %get-tuple-element.95), channel_id=1, source_target_pairs={{0,1},{1,0},{2,3},{3,2},{4,5},{5,4},{6,7},{7,6},{8,9},{9,8},{10,11... | collective-permute-start | bytes 1572872 | tf_op jit(solution)/shard_map/ppermute | solution.py:19
  34.0 3.6 %collective-permute-start.12 = (bf16[64,2048]{1,0:T(8,128)(2,1)S(1)}, bf16[64,2048]{1,0:T(8,128)(2,1)S(1)}, u32[]{:S(2)}, u32[]{:S(2)}) collective-permute-start(bf16[64,2048]{1,0:T(8,128)(2,1)S(1)} %collective-permute-done.8.mine_ref.refs_22_), channel_id=1, source_target_pairs={{0,1},{1,0},{2,3},{3,2},{4,5},{5,4},{6,7},{7,6},{8,9},{9,8},{10,11... | collective-permute-start | bytes 786440 | tf_op jit(solution)/shard_map/ppermute | solution.py:19
  34.9 9.8 %collective-permute-start.6 = (bf16[64,2048]{1,0:T(8,128)(2,1)S(1)}, bf16[64,2048]{1,0:T(8,128)(2,1)S(1)}, u32[]{:S(2)}, u32[]{:S(2)}) collective-permute-start(bf16[64,2048]{1,0:T(8,128)(2,1)S(1)} %slice_add_fusion.3), channel_id=1, source_target_pairs={{0,2},{1,3},{2,4},{3,5},{4,6},{5,7},{6,0},{7,1},{8,10},{9,11},{10,... | collective-permute-start | bytes 786440 | tf_op jit(solution)/shard_map/ppermute | solution.py:24
  36.0 9.3 %collective-permute-start.10 = (bf16[64,2048]{1,0:T(8,128)(2,1)S(1)}, bf16[64,2048]{1,0:T(8,128)(2,1)S(1)}, u32[]{:S(2)}, u32[]{:S(2)}) collective-permute-start(bf16[64,2048]{1,0:T(8,128)(2,1)S(1)} %slice.66), channel_id=1, source_target_pairs={{0,8},{8,16},{16,24},{24,0},{1,9},{9,17},{17,25},{25,1},{2,10},{10... | collective-permute-start | bytes 786440 | tf_op jit(solution)/shard_map/ppermute | solution.py:29
  45.4 2.0 %collective-permute-start.13 = (bf16[64,4096]{1,0:T(8,128)(2,1)S(1)}, bf16[64,4096]{1,0:T(8,128)(2,1)S(1)}, u32[]{:S(2)}, u32[]{:S(2)}) collective-permute-start(bf16[64,4096]{1,0:T(8,128)(2,1)S(1)} %get-tuple-element.102), channel_id=1, source_target_pairs={{0,1},{1,0},{2,3},{3,2},{4,5},{5,4},{6,7},{7,6},{8,9},{9,8},{10,11... | collective-permute-start | bytes 1572872 | tf_op jit(solution)/shard_map/ppermute | solution.py:19
  45.5 10.5 %collective-permute-start.11 = (bf16[64,2048]{1,0:T(8,128)(2,1)S(1)}, bf16[64,2048]{1,0:T(8,128)(2,1)S(1)}, u32[]{:S(2)}, u32[]{:S(2)}) collective-permute-start(bf16[64,2048]{1,0:T(8,128)(2,1)S(1)} %fusion.5), channel_id=1, source_target_pairs={{0,2},{1,3},{2,4},{3,5},{4,6},{5,7},{6,0},{7,1},{8,10},{9,11},{10,... | collective-permute-start | bytes 786440 | tf_op jit(solution)/shard_map/ppermute | solution.py:24
  47.5 9.8 %slice-start = ((s8[8388608]{0:T(1024)(128)(4,1)}), s8[4194304]{0:T(1024)(128)(4,1)S(1)}, s32[]{:S(2)}) async-start(s8[8388608]{0:T(1024)(128)(4,1)} %bitcast.8), calls=%async_computation | async-start | bytes 8388608
  47.6 9.7 %slice-start.1 = ((s8[8388608]{0:T(1024)(128)(4,1)}), s8[4194304]{0:T(1024)(128)(4,1)S(1)}, s32[]{:S(2)}) async-start(s8[8388608]{0:T(1024)(128)(4,1)} %bitcast.8), calls=%async_computation.1 | async-start | bytes 8388608
  47.6 9.3 %collective-permute-start.14 = (bf16[64,2048]{1,0:T(8,128)(2,1)S(1)}, bf16[64,2048]{1,0:T(8,128)(2,1)S(1)}, u32[]{:S(2)}, u32[]{:S(2)}) collective-permute-start(bf16[64,2048]{1,0:T(8,128)(2,1)S(1)} %slice.65), channel_id=1, source_target_pairs={{0,8},{8,16},{16,24},{24,0},{1,9},{9,17},{17,25},{25,1},{2,10},{10... | collective-permute-start | bytes 786440 | tf_op jit(solution)/shard_map/ppermute | solution.py:29
  48.5 8.5 %collective-permute-start.16 = (bf16[64,4096]{1,0:T(8,128)(2,1)S(1)}, bf16[64,4096]{1,0:T(8,128)(2,1)S(1)}, u32[]{:S(2)}, u32[]{:S(2)}) collective-permute-start(bf16[64,4096]{1,0:T(8,128)(2,1)S(1)} %get-tuple-element.88), channel_id=1, source_target_pairs={{0,1},{1,0},{2,3},{3,2},{4,5},{5,4},{6,7},{7,6},{8,9},{9,8},{10,11... | collective-permute-start | bytes 1572872 | tf_op jit(solution)/shard_map/ppermute | solution.py:19
  57.0 9.4 %collective-permute-start.15 = (bf16[64,2048]{1,0:T(8,128)(2,1)S(1)}, bf16[64,2048]{1,0:T(8,128)(2,1)S(1)}, u32[]{:S(2)}, u32[]{:S(2)}) collective-permute-start(bf16[64,2048]{1,0:T(8,128)(2,1)S(1)} %fusion.4), channel_id=1, source_target_pairs={{0,2},{1,3},{2,4},{3,5},{4,6},{5,7},{6,0},{7,1},{8,10},{9,11},{10,... | collective-permute-start | bytes 786440 | tf_op jit(solution)/shard_map/ppermute | solution.py:24
  57.2 9.2 %copy-start.3 = (bf16[1,64,2048]{2,1,0:T(8,128)(2,1)S(1)}, bf16[1,64,2048]{2,1,0:T(8,128)(2,1)}, u32[]{:S(2)}) copy-start(bf16[1,64,2048]{2,1,0:T(8,128)(2,1)} %param.7) | copy-start | bytes 786436
  57.2 9.2 %copy-start.4 = (f32[1,2048]{1,0:T(1,128)S(1)}, f32[1,2048]{1,0:T(1,128)}, u32[]{:S(2)}) copy-start(f32[1,2048]{1,0:T(1,128)} %param.11) | copy-start | bytes 24580
  57.2 9.1 %collective-permute-start.17 = (bf16[64,2048]{1,0:T(8,128)(2,1)S(1)}, bf16[64,2048]{1,0:T(8,128)(2,1)S(1)}, u32[]{:S(2)}, u32[]{:S(2)}) collective-permute-start(bf16[64,2048]{1,0:T(8,128)(2,1)S(1)} %slice.64), channel_id=1, source_target_pairs={{0,8},{8,16},{16,24},{24,0},{1,9},{9,17},{17,25},{25,1},{2,10},{10... | collective-permute-start | bytes 786440 | tf_op jit(solution)/shard_map/ppermute | solution.py:29
  66.6 1.7 %collective-permute-start.18 = (bf16[64,2048]{1,0:T(8,128)(2,1)S(1)}, bf16[64,2048]{1,0:T(8,128)(2,1)S(1)}, u32[]{:S(2)}, u32[]{:S(2)}) collective-permute-start(bf16[64,2048]{1,0:T(8,128)(2,1)S(1)} %fusion.3.refs_2_.refs_12_), channel_id=1, source_target_pairs={{0,1},{1,0},{2,3},{3,2},{4,5},{5,4},{6,7},{7,6},{8,9},{9,8},{10,11... | collective-permute-start | bytes 786440 | tf_op jit(solution)/shard_map/ppermute | solution.py:19
  66.6 10.5 %collective-permute-start.20 = (bf16[64,2048]{1,0:T(8,128)(2,1)S(1)}, bf16[64,2048]{1,0:T(8,128)(2,1)S(1)}, u32[]{:S(2)}, u32[]{:S(2)}) collective-permute-start(bf16[64,2048]{1,0:T(8,128)(2,1)S(1)} %fusion.3.refs_2_.refs_12_), channel_id=1, source_target_pairs={{0,2},{1,3},{2,4},{3,5},{4,6},{5,7},{6,0},{7,1},{8,10},{9,11},{10,... | collective-permute-start | bytes 786440 | tf_op jit(solution)/shard_map/ppermute | solution.py:24
  67.3 9.9 %collective-permute-start.24 = (bf16[64,2048]{1,0:T(8,128)(2,1)S(1)}, bf16[64,2048]{1,0:T(8,128)(2,1)S(1)}, u32[]{:S(2)}, u32[]{:S(2)}) collective-permute-start(bf16[64,2048]{1,0:T(8,128)(2,1)S(1)} %fusion.3.refs_2_.refs_12_), channel_id=1, source_target_pairs={{0,24},{8,0},{16,8},{24,16},{1,25},{9,1},{17,9},{25,17},{2,26},{10... | collective-permute-start | bytes 786440 | tf_op jit(solution)/shard_map/ppermute | solution.py:29
  77.2 5.7 %collective-permute-start.25 = (bf16[64,2048]{1,0:T(8,128)(2,1)S(1)}, bf16[64,2048]{1,0:T(8,128)(2,1)S(1)}, u32[]{:S(2)}, u32[]{:S(2)}) collective-permute-start(bf16[64,2048]{1,0:T(8,128)(2,1)S(1)} %broadcast_select_fusion.3.refs_4_.refs_10_), channel_id=1, source_target_pairs={{0,1},{1,0},{2,3},{3,2},{4,5},{5,4},{6,7},{7,6},{8,9},{9,8},{10,11... | collective-permute-start | bytes 786440 | tf_op jit(solution)/shard_map/ppermute | solution.py:19
  77.3 5.6 %collective-permute-start.23 = (bf16[64,2048]{1,0:T(8,128)(2,1)S(1)}, bf16[64,2048]{1,0:T(8,128)(2,1)S(1)}, u32[]{:S(2)}, u32[]{:S(2)}) collective-permute-start(bf16[64,2048]{1,0:T(8,128)(2,1)S(1)} %collective-permute-done.20.refs_2_.refs_14_), channel_id=1, source_target_pairs={{0,1},{1,0},{2,3},{3,2},{4,5},{5,4},{6,7},{7,6},{8,9},{9,8},{10,11... | collective-permute-start | bytes 786440 | tf_op jit(solution)/shard_map/ppermute | solution.py:19
  77.8 10.4 %collective-permute-start.22 = (bf16[64,2048]{1,0:T(8,128)(2,1)S(1)}, bf16[64,2048]{1,0:T(8,128)(2,1)S(1)}, u32[]{:S(2)}, u32[]{:S(2)}) collective-permute-start(bf16[64,2048]{1,0:T(8,128)(2,1)S(1)} %collective-permute-done.20.refs_2_.refs_14_), channel_id=1, source_target_pairs={{0,2},{1,3},{2,4},{3,5},{4,6},{5,7},{6,0},{7,1},{8,10},{9,11},{10,... | collective-permute-start | bytes 786440 | tf_op jit(solution)/shard_map/ppermute | solution.py:24
  78.0 10.1 %collective-permute-start.21 = (bf16[64,2048]{1,0:T(8,128)(2,1)S(1)}, bf16[64,2048]{1,0:T(8,128)(2,1)S(1)}, u32[]{:S(2)}, u32[]{:S(2)}) collective-permute-start(bf16[64,2048]{1,0:T(8,128)(2,1)S(1)} %collective-permute-done.20.refs_2_.refs_14_), channel_id=1, source_target_pairs={{0,24},{8,0},{16,8},{24,16},{1,25},{9,1},{17,9},{25,17},{2,26},{10... | collective-permute-start | bytes 786440 | tf_op jit(solution)/shard_map/ppermute | solution.py:29
  79.3 8.9 %collective-permute-start.27 = (f32[1,2048]{1,0:T(1,128)S(1)}, f32[1,2048]{1,0:T(1,128)S(1)}, u32[]{:S(2)}, u32[]{:S(2)}) collective-permute-start(f32[1,2048]{1,0:T(1,128)S(1)} %get-tuple-element.106), channel_id=1, source_target_pairs={{0,6},{1,7},{2,0},{3,1},{4,2},{5,3},{6,4},{7,5},{8,14},{9,15},{10,... | collective-permute-start | bytes 24584 | tf_op jit(solution)/shard_map/ppermute | solution.py:24
  82.9 5.6 %collective-permute-start.26 = (f32[1,2048]{1,0:T(1,128)S(1)}, f32[1,2048]{1,0:T(1,128)S(1)}, u32[]{:S(2)}, u32[]{:S(2)}) collective-permute-start(f32[1,2048]{1,0:T(1,128)S(1)} %get-tuple-element.106), channel_id=1, source_target_pairs={{0,4},{1,5},{2,6},{3,7},{4,0},{5,1},{6,2},{7,3},{8,12},{9,13},{10,... | collective-permute-start | bytes 24584 | tf_op jit(solution)/shard_map/ppermute | solution.py:24
  82.9 5.6 %collective-permute-start.19 = (f32[1,2048]{1,0:T(1,128)S(1)}, f32[1,2048]{1,0:T(1,128)S(1)}, u32[]{:S(2)}, u32[]{:S(2)}) collective-permute-start(f32[1,2048]{1,0:T(1,128)S(1)} %get-tuple-element.106), channel_id=1, source_target_pairs={{0,2},{1,3},{2,4},{3,5},{4,6},{5,7},{6,0},{7,1},{8,10},{9,11},{10,... | collective-permute-start | bytes 24584 | tf_op jit(solution)/shard_map/ppermute | solution.py:24
  88.6 4.0 %collective-permute-start.32 = (bf16[64,2048]{1,0:T(8,128)(2,1)S(1)}, bf16[64,2048]{1,0:T(8,128)(2,1)S(1)}, u32[]{:S(2)}, u32[]{:S(2)}) collective-permute-start(bf16[64,2048]{1,0:T(8,128)(2,1)S(1)} %broadcast_select_fusion.2.refs_4_.refs_12_), channel_id=1, source_target_pairs={{0,1},{1,0},{2,3},{3,2},{4,5},{5,4},{6,7},{7,6},{8,9},{9,8},{10,11... | collective-permute-start | bytes 786440 | tf_op jit(solution)/shard_map/ppermute | solution.py:19
  88.7 5.1 %collective-permute-start.31 = (bf16[64,2048]{1,0:T(8,128)(2,1)S(1)}, bf16[64,2048]{1,0:T(8,128)(2,1)S(1)}, u32[]{:S(2)}, u32[]{:S(2)}) collective-permute-start(bf16[64,2048]{1,0:T(8,128)(2,1)S(1)} %collective-permute-done.22.refs_2_.refs_16_), channel_id=1, source_target_pairs={{0,1},{1,0},{2,3},{3,2},{4,5},{5,4},{6,7},{7,6},{8,9},{9,8},{10,11... | collective-permute-start | bytes 786440 | tf_op jit(solution)/shard_map/ppermute | solution.py:19
  89.1 10.1 %collective-permute-start.30 = (bf16[64,2048]{1,0:T(8,128)(2,1)S(1)}, bf16[64,2048]{1,0:T(8,128)(2,1)S(1)}, u32[]{:S(2)}, u32[]{:S(2)}) collective-permute-start(bf16[64,2048]{1,0:T(8,128)(2,1)S(1)} %collective-permute-done.22.refs_2_.refs_16_), channel_id=1, source_target_pairs={{0,2},{1,3},{2,4},{3,5},{4,6},{5,7},{6,0},{7,1},{8,10},{9,11},{10,... | collective-permute-start | bytes 786440 | tf_op jit(solution)/shard_map/ppermute | solution.py:24
  90.2 9.0 %collective-permute-start.29 = (bf16[64,2048]{1,0:T(8,128)(2,1)S(1)}, bf16[64,2048]{1,0:T(8,128)(2,1)S(1)}, u32[]{:S(2)}, u32[]{:S(2)}) collective-permute-start(bf16[64,2048]{1,0:T(8,128)(2,1)S(1)} %collective-permute-done.22.refs_2_.refs_16_), channel_id=1, source_target_pairs={{0,24},{8,0},{16,8},{24,16},{1,25},{9,1},{17,9},{25,17},{2,26},{10... | collective-permute-start | bytes 786440 | tf_op jit(solution)/shard_map/ppermute | solution.py:29
  91.9 7.4 %collective-permute-start.34 = (f32[1,2048]{1,0:T(1,128)S(1)}, f32[1,2048]{1,0:T(1,128)S(1)}, u32[]{:S(2)}, u32[]{:S(2)}) collective-permute-start(f32[1,2048]{1,0:T(1,128)S(1)} %add_add_fusion.1), channel_id=1, source_target_pairs={{0,24},{8,0},{16,8},{24,16},{1,25},{9,1},{17,9},{25,17},{2,26},{10... | collective-permute-start | bytes 24584 | tf_op jit(solution)/shard_map/ppermute | solution.py:29
  92.6 6.7 %collective-permute-start.33 = (f32[1,2048]{1,0:T(1,128)S(1)}, f32[1,2048]{1,0:T(1,128)S(1)}, u32[]{:S(2)}, u32[]{:S(2)}) collective-permute-start(f32[1,2048]{1,0:T(1,128)S(1)} %add_add_fusion.1), channel_id=1, source_target_pairs={{0,16},{8,24},{16,0},{24,8},{1,17},{9,25},{17,1},{25,9},{2,18},{10... | collective-permute-start | bytes 24584 | tf_op jit(solution)/shard_map/ppermute | solution.py:29
  93.7 5.5 %collective-permute-start.28 = (f32[1,2048]{1,0:T(1,128)S(1)}, f32[1,2048]{1,0:T(1,128)S(1)}, u32[]{:S(2)}, u32[]{:S(2)}) collective-permute-start(f32[1,2048]{1,0:T(1,128)S(1)} %add_add_fusion.1), channel_id=1, source_target_pairs={{0,8},{8,16},{16,24},{24,0},{1,9},{9,17},{17,25},{25,1},{2,10},{10... | collective-permute-start | bytes 24584 | tf_op jit(solution)/shard_map/ppermute | solution.py:29
  99.9 2.4 %collective-permute-start.36 = (bf16[64,2048]{1,0:T(8,128)(2,1)S(1)}, bf16[64,2048]{1,0:T(8,128)(2,1)S(1)}, u32[]{:S(2)}, u32[]{:S(2)}) collective-permute-start(bf16[64,2048]{1,0:T(8,128)(2,1)S(1)} %collective-permute-done.30.refs_2_), channel_id=1, source_target_pairs={{0,1},{1,0},{2,3},{3,2},{4,5},{5,4},{6,7},{7,6},{8,9},{9,8},{10,11... | collective-permute-start | bytes 786440 | tf_op jit(solution)/shard_map/ppermute | solution.py:19
  99.9 2.4 %collective-permute-start.37 = (bf16[64,2048]{1,0:T(8,128)(2,1)S(1)}, bf16[64,2048]{1,0:T(8,128)(2,1)S(1)}, u32[]{:S(2)}, u32[]{:S(2)}) collective-permute-start(bf16[64,2048]{1,0:T(8,128)(2,1)S(1)} %broadcast_select_fusion.1.refs_4_.refs_14_), channel_id=1, source_target_pairs={{0,1},{1,0},{2,3},{3,2},{4,5},{5,4},{6,7},{7,6},{8,9},{9,8},{10,11... | collective-permute-start | bytes 786440 | tf_op jit(solution)/shard_map/ppermute | solution.py:19
  100.4 11.6 %collective-permute-start.35 = (bf16[64,2048]{1,0:T(8,128)(2,1)S(1)}, bf16[64,2048]{1,0:T(8,128)(2,1)S(1)}, u32[]{:S(2)}, u32[]{:S(2)}) collective-permute-start(bf16[64,2048]{1,0:T(8,128)(2,1)S(1)} %collective-permute-done.30.refs_2_), channel_id=1, source_target_pairs={{0,24},{8,0},{16,8},{24,16},{1,25},{9,1},{17,9},{25,17},{2,26},{10... | collective-permute-start | bytes 786440 | tf_op jit(solution)/shard_map/ppermute | solution.py:29
  102.3 11.4 %copy-start.1 = (bf16[1,64,2048]{2,1,0:T(8,128)(2,1)S(1)}, bf16[1,64,2048]{2,1,0:T(8,128)(2,1)}, u32[]{:S(2)}) copy-start(bf16[1,64,2048]{2,1,0:T(8,128)(2,1)} %param.6) | copy-start | bytes 786436
  112.1 1.6 %collective-permute-start.38 = (bf16[64,2048]{1,0:T(8,128)(2,1)S(1)}, bf16[64,2048]{1,0:T(8,128)(2,1)S(1)}, u32[]{:S(2)}, u32[]{:S(2)}) collective-permute-start(bf16[64,2048]{1,0:T(8,128)(2,1)S(1)} %broadcast_select_fusion.refs_2_), channel_id=1, source_target_pairs={{0,1},{1,0},{2,3},{3,2},{4,5},{5,4},{6,7},{7,6},{8,9},{9,8},{10,11... | collective-permute-start | bytes 786440 | tf_op jit(solution)/shard_map/ppermute | solution.py:19
where the time goes:
time: 128 us
  Pallas kernels  61.9 us (48%)
  waiting for transfers between devices  36 us (28%)
  starting transfers between devices  26.7 us (21%)
  other arithmetic  1.61 us (1%)
    pallas_call x12, Pallas kernels, call(): pl.pallas_call(kernel, in_specs=in_specs or [VMEM] * len(args), out_specs...  61.9 us
    ppermute x12, waiting for transfers between devices, from_below(): lax.ppermute(block, 'feat', [(i, (i + 2 * distance) % size) for i in rang...  28 us
    ppermute x11, starting transfers between devices, round_layers(): lax.ppermute(block, 'layer', [(i, (i + distance) % size) for i in range(s...  12.4 us
    ppermute x12, starting transfers between devices, from_below(): lax.ppermute(block, 'feat', [(i, (i + 2 * distance) % size) for i in rang...  10.9 us
    ppermute x16, waiting for transfers between devices, swapped(): return lax.ppermute(block, 'feat', [(i, i ^ 1) for i in range(size)])  6.12 us
    ppermute x16, starting transfers between devices, swapped(): return lax.ppermute(block, 'feat', [(i, i ^ 1) for i in range(size)])  3.41 us
  transfers between devices with their start and end apart: 39, of which 18 were waited for; matrix products, arithmetic and copies ran while one was open for 1% of the time, Pallas kernels for 38%

commit v1 on v0

--- a/solution.py
+++ b/solution.py
@@ -372,11 +372,17 @@
         jobs = []
         if j == chips - 2:
             jobs = [(acts, [part for pair in here for part in pair], 2, 0)]
-        (back,), (dpre,), acc = backward(
-            decoders_t, [here[j + 1]], [(later[j], back, pres[j])], acc[:2], jobs
-        )
+        second = later[j], back, pres[j]
+        if jobs:
+            (back,), _, (*acc, dec_grad) = backward(decoders_t, [here[j + 1]], [], acc[:2], jobs)
+            pair, *second = second
+            second = (after(pair[0], back), pair[1]), *second
+            _, (dpre,), acc = backward(decoders_t, [], [second], acc[:2])
+            done = back
+        else:
+            (back,), (dpre,), acc = backward(decoders_t, [here[j + 1]], [second], acc[:2])
+            done = dpre
         dpres.append(dpre)
-        done, dec_grad = dpre, acc[-1]
 
     flat = [part for pair in tokens for part in pair]
     jobs = [(acts, [part for pair in later for part in pair], 2, 1), (flat, [*dpres, 0], 1, 0)]

time: 128 us -> 126 us (0.984)
  waiting for transfers between devices: 36 us -> 34.5 us
    ppermute x16, waiting for transfers between devices: 6.12 us -> 4.63 us  [swapped(): return lax.ppermute(block, 'feat', [(i, i ^ 1) for i in range(size)])]
    pallas_call x12 -> x13, Pallas kernels: 61.9 us -> 62 us  [call(): pl.pallas_call(kernel, in_specs=in_specs or [VMEM] * len(args), out_specs...]
  transfers between devices with their start and end apart: 39 -> 39, of which waited for: 18 -> 17; matrix products, arithmetic and copies ran while one was open for 1% -> 1% of each run, Pallas kernels for 38% -> 38%
where the time goes in v1:
time: 126 us
  Pallas kernels  62 us (49%)
  waiting for transfers between devices  34.5 us (27%)
  starting transfers between devices  26.6 us (21%)
  other arithmetic  1.64 us (1%)
    pallas_call x13, Pallas kernels, call(): pl.pallas_call(kernel, in_specs=in_specs or [VMEM] * len(args), out_specs...  62 us
    ppermute x12, waiting for transfers between devices, from_below(): lax.ppermute(block, 'feat', [(i, (i + 2 * distance) % size) for i in rang...  28.1 us
    ppermute x11, starting transfers between devices, round_layers(): lax.ppermute(block, 'layer', [(i, (i + distance) % size) for i in range(s...  12.3 us
    ppermute x12, starting transfers between devices, from_below(): lax.ppermute(block, 'feat', [(i, (i + 2 * distance) % size) for i in rang...  10.9 us
    ppermute x16, waiting for transfers between devices, swapped(): return lax.ppermute(block, 'feat', [(i, i ^ 1) for i in range(size)])  4.63 us
    ppermute x16, starting transfers between devices, swapped(): return lax.ppermute(block, 'feat', [(i, i ^ 1) for i in range(size)])  3.4 us
  transfers between devices with their start and end apart: 39, of which 17 were waited for; matrix products, arithmetic and copies ran while one was open for 1% of the time, Pallas kernels for 38%

profile of v1, /device:TPU:0, one launch (start us, length us, event | category | flops | bytes accessed | tf_op | source)
XLA Modules:
  0.0 126.2 jit_solution(8536627559558313911)
XLA Ops:
  0.6 0.5 collective-permute-start
  1.2 2.6 %collective-permute-start.1 = (bf16[64,2048]{1,0:T(8,128)(2,1)}, bf16[64,2048]{1,0:T(8,128)(2,1)S(1)}, u32[]{:S(2)}, u32[]{:S(2)}) collective-permute-start(bf16[64,2048]{1,0:T(8,128)(2,1)} %bitcast.11), channel_id=1, source_target_pairs={{0,2},{1,3},{2,4},{3,5},{4,6},{5,7},{6,0},{7,1},{8,10},{9,11},{10,... | collective-permute-start | bytes 786440 | tf_op jit(solution)/shard_map/ppermute | solution.py:24
  3.8 8.3 %prepared.1 = (f32[128,2048]{1,0:T(8,128)S(1)}, bf16[128,2048]{1,0:T(8,128)(2,1)S(1)}, bf16[2048,2048]{1,0:T(8,128)(2,1)S(1)}, bf16[2048,2048]{1,0:T(8,128)(2,1)S(1)}, bf16[2048,2048]{1,0:T(8,128)(2,1)S(1)}) custom-call(bf16[64,2048]{1,0:T(8,128)(2,1)} %bitcast.12, bf16[64,2048]{1,0:T(8,128)(2,1)S(1)} %collective-permute-done.theirs_ref.refs_17_, ...), custom_call_target="tpu_custom_call" | custom-call | flops 1073741824 | bytes 52436992 | tf_op jit(solution)/shard_map/prepared/pallas_call | solution.py:42
  12.2 0.8 collective-permute-done.1.mine_ref.refs_18_
  13.0 1.1 collective-permute-start.3
  14.1 0.4 collective-permute-done.2.theirs_ref.refs_19_
  14.5 4.5 %chunk.3 = (f32[128,2048]{1,0:T(8,128)S(1)}, bf16[128,2048]{1,0:T(8,128)(2,1)S(1)}, f32[64,4096]{1,0:T(8,128)S(1)}, bf16[64,4096]{1,0:T(8,128)(2,1)S(1)}) custom-call(bf16[64,2048]{1,0:T(8,128)(2,1)S(1)} %collective-permute-done.1.mine_ref.refs_18_, bf16[64,2048]{1,0:T(8,128)(2,1)S(1)} %collective-permute-done.2.theirs_ref.refs_19_, ...), custom_call_target="tpu_custom_call" | custom-call | flops 3221225472 | bytes 28844032 | tf_op jit(solution)/shard_map/chunk/pallas_call | solution.py:42
  19.0 2.9 %decoded.1 = (f32[64,4096]{1,0:T(8,128)S(1)}, bf16[64,4096]{1,0:T(8,128)(2,1)S(1)}) custom-call(bf16[128,2048]{1,0:T(8,128)(2,1)S(1)} %get-tuple-element.90.act_ref.refs_4_.refs_6_, bf16[2048,2048]{1,0:T(8,128)(2,1)S(1)} %get-tuple-element.99.refs_0_.weight_ref, bf16[2048,2048]{1,0:T(8,128)(2,1)S(1)} %get-tuple-element.106.refs_1_.weight_ref), custom_call_target="tpu_custom_call" | custom-call | flops 2147483648 | bytes 18874368 | tf_op jit(solution)/shard_map/decoded/pallas_call | solution.py:42
  22.0 1.5 %collective-permute-done.3.mine_ref.refs_20_ = bf16[64,2048]{1,0:T(8,128)(2,1)S(1)} collective-permute-done((bf16[64,2048]{1,0:T(8,128)(2,1)S(1)}, bf16[64,2048]{1,0:T(8,128)(2,1)S(1)}, u32[]{:S(2)}, u32[]{:S(2)}) %collective-permute-start.3) | collective-permute-done | bytes 262176 | tf_op jit(solution)/shard_map/ppermute | solution.py:24
  23.5 0.5 collective-permute-start.7
  24.0 1.4 %collective-permute-done.4 = bf16[64,4096]{1,0:T(8,128)(2,1)S(1)} collective-permute-done((bf16[64,4096]{1,0:T(8,128)(2,1)S(1)}, bf16[64,4096]{1,0:T(8,128)(2,1)S(1)}, u32[]{:S(2)}, u32[]{:S(2)}) %collective-permute-start.4) | collective-permute-done | bytes 524320 | tf_op jit(solution)/shard_map/ppermute | solution.py:19
  25.4 0.1 convert_add_fusion.3
  25.5 1.5 %collective-permute-start.5 = (bf16[64,2048]{1,0:T(8,128)(2,1)S(1)}, bf16[64,2048]{1,0:T(8,128)(2,1)S(1)}, u32[]{:S(2)}, u32[]{:S(2)}) collective-permute-start(bf16[64,2048]{1,0:T(8,128)(2,1)S(1)} %slice.67), channel_id=1, source_target_pairs={{0,8},{8,16},{16,24},{24,0},{1,9},{9,17},{17,25},{25,1},{2,10},{10... | collective-permute-start | bytes 786440 | tf_op jit(solution)/shard_map/ppermute | solution.py:29
  27.1 4.5 %chunk.4 = (f32[128,2048]{1,0:T(8,128)S(1)}, bf16[128,2048]{1,0:T(8,128)(2,1)S(1)}, f32[64,4096]{1,0:T(8,128)S(1)}, bf16[64,4096]{1,0:T(8,128)(2,1)S(1)}) custom-call(bf16[64,2048]{1,0:T(8,128)(2,1)S(1)} %collective-permute-done.3.mine_ref.refs_20_, bf16[64,2048]{1,0:T(8,128)(2,1)S(1)} %collective-permute-done.7.theirs_ref.refs_21_, ...), custom_call_target="tpu_custom_call" | custom-call | flops 3221225472 | bytes 28844032 | tf_op jit(solution)/shard_map/chunk/pallas_call | solution.py:42
  31.6 2.4 %collective-permute-done.8.mine_ref.refs_22_ = bf16[64,2048]{1,0:T(8,128)(2,1)S(1)} collective-permute-done((bf16[64,2048]{1,0:T(8,128)(2,1)S(1)}, bf16[64,2048]{1,0:T(8,128)(2,1)S(1)}, u32[]{:S(2)}, u32[]{:S(2)}) %collective-permute-start.8) | collective-permute-done | bytes 262176 | tf_op jit(solution)/shard_map/ppermute | solution.py:24
  34.0 0.5 collective-permute-start.12
  34.5 0.3 collective-permute-done.5
  34.8 0.1 slice_add_fusion.3
  35.0 0.9 collective-permute-done.9
  35.9 0.1 convert_add_fusion.2
  36.1 1.5 %collective-permute-start.10 = (bf16[64,2048]{1,0:T(8,128)(2,1)S(1)}, bf16[64,2048]{1,0:T(8,128)(2,1)S(1)}, u32[]{:S(2)}, u32[]{:S(2)}) collective-permute-start(bf16[64,2048]{1,0:T(8,128)(2,1)S(1)} %slice.66), channel_id=1, source_target_pairs={{0,8},{8,16},{16,24},{24,0},{1,9},{9,17},{17,25},{25,1},{2,10},{10... | collective-permute-start | bytes 786440 | tf_op jit(solution)/shard_map/ppermute | solution.py:29
  37.6 4.5 %chunk.5 = (f32[128,2048]{1,0:T(8,128)S(1)}, bf16[128,2048]{1,0:T(8,128)(2,1)S(1)}, f32[64,4096]{1,0:T(8,128)S(1)}, bf16[64,4096]{1,0:T(8,128)(2,1)S(1)}) custom-call(bf16[64,2048]{1,0:T(8,128)(2,1)S(1)} %collective-permute-done.8.mine_ref.refs_22_, bf16[64,2048]{1,0:T(8,128)(2,1)S(1)} %collective-permute-done.12.theirs_ref.refs_23_, ...), custom_call_target="tpu_custom_call" | custom-call | flops 3221225472 | bytes 28844032 | tf_op jit(solution)/shard_map/chunk/pallas_call | solution.py:42
  42.2 2.6 %collective-permute-done.6 = bf16[64,2048]{1,0:T(8,128)(2,1)S(1)} collective-permute-done((bf16[64,2048]{1,0:T(8,128)(2,1)S(1)}, bf16[64,2048]{1,0:T(8,128)(2,1)S(1)}, u32[]{:S(2)}, u32[]{:S(2)}) %collective-permute-start.6) | collective-permute-done | bytes 262176 | tf_op jit(solution)/shard_map/ppermute | solution.py:24
  44.7 0.6 collective-permute-done.10
  45.4 0.1 fusion.5
  45.6 1.8 %collective-permute-done.13 = bf16[64,4096]{1,0:T(8,128)(2,1)S(1)} collective-permute-done((bf16[64,4096]{1,0:T(8,128)(2,1)S(1)}, bf16[64,4096]{1,0:T(8,128)(2,1)S(1)}, u32[]{:S(2)}, u32[]{:S(2)}) %collective-permute-start.13) | collective-permute-done | bytes 524320 | tf_op jit(solution)/shard_map/ppermute | solution.py:19
  47.5 0.1 convert_add_fusion.1
  47.6 0.9 collective-permute-start.14
  48.5 2.8 %transposed.2.refs_0_ = bf16[2048,2048]{1,0:T(8,128)(2,1)S(1)} custom-call(bf16[2048,2048]{1,0:T(8,128)(2,1)S(1)} %get-tuple-element.99.refs_0_.weight_ref), custom_call_target="tpu_custom_call" | custom-call | flops 1073741824 | bytes 16777216 | tf_op jit(solution)/shard_map/transposed/pallas_call | solution.py:42
  51.4 4.7 %collective-permute-done.11 = bf16[64,2048]{1,0:T(8,128)(2,1)S(1)} collective-permute-done((bf16[64,2048]{1,0:T(8,128)(2,1)S(1)}, bf16[64,2048]{1,0:T(8,128)(2,1)S(1)}, u32[]{:S(2)}, u32[]{:S(2)}) %collective-permute-start.11) | collective-permute-done | bytes 262176 | tf_op jit(solution)/shard_map/ppermute | solution.py:24
  56.1 0.9 collective-permute-done.14
  56.9 0.1 fusion.4
  57.1 0.1 convert_add_fusion
  57.4 2.8 %transposed.3.refs_1_ = bf16[2048,2048]{1,0:T(8,128)(2,1)S(1)} custom-call(bf16[2048,2048]{1,0:T(8,128)(2,1)S(1)} %bitcast.9), custom_call_target="tpu_custom_call" | custom-call | flops 1073741824 | bytes 16777216 | tf_op jit(solution)/shard_map/transposed/pallas_call | solution.py:42
  60.2 6.2 %collective-permute-done.15 = bf16[64,2048]{1,0:T(8,128)(2,1)S(1)} collective-permute-done((bf16[64,2048]{1,0:T(8,128)(2,1)S(1)}, bf16[64,2048]{1,0:T(8,128)(2,1)S(1)}, u32[]{:S(2)}, u32[]{:S(2)}) %collective-permute-start.15) | collective-permute-done | bytes 262176 | tf_op jit(solution)/shard_map/ppermute | solution.py:24
  66.4 0.2 fusion.3.refs_2_.refs_8_
  66.7 0.6 collective-permute-start.20
  67.3 1.0 collective-permute-start.24
  68.3 1.7 %backward.6 = (f32[128,2048]{1,0:T(8,128)S(1)}, f32[1,2048]{1,0:T(1,128)S(1)}, f32[1,2048]{1,0:T(1,128)S(1)}, f32[1,2048]{1,0:T(1,128)S(1)}) custom-call(bf16[2048,2048]{1,0:T(8,128)(2,1)S(1)} %transposed.2.refs_0_, bf16[2048,2048]{1,0:T(8,128)(2,1)S(1)} %transposed.3.refs_1_, bf16[64,2048]{1,0:T(8,128)(2,1)S(1)} %fusion.3.refs_2_.refs_8_, ...), custom_call_target="tpu_custom_call" | custom-call | flops 1073741824 | bytes 18374656 | tf_op jit(solution)/shard_map/backward/pallas_call | solution.py:42
  70.0 7.2 %collective-permute-done.20.refs_2_.refs_10_ = bf16[64,2048]{1,0:T(8,128)(2,1)S(1)} collective-permute-done((bf16[64,2048]{1,0:T(8,128)(2,1)S(1)}, bf16[64,2048]{1,0:T(8,128)(2,1)S(1)}, u32[]{:S(2)}, u32[]{:S(2)}) %collective-permute-start.20) | collective-permute-done | bytes 262176 | tf_op jit(solution)/shard_map/ppermute | solution.py:24
  77.3 0.5 collective-permute-start.23
  77.8 0.3 collective-permute-start.22
  78.1 1.2 collective-permute-start.21
  79.4 3.6 %collective-permute-start.27 = (f32[1,2048]{1,0:T(1,128)S(1)}, f32[1,2048]{1,0:T(1,128)S(1)}, u32[]{:S(2)}, u32[]{:S(2)}) collective-permute-start(f32[1,2048]{1,0:T(1,128)S(1)} %get-tuple-element.109), channel_id=1, source_target_pairs={{0,6},{1,7},{2,0},{3,1},{4,2},{5,3},{6,4},{7,5},{8,14},{9,15},{10,... | collective-permute-start | bytes 24584 | tf_op jit(solution)/shard_map/ppermute | solution.py:24
  82.9 1.4 %collective-permute-start.19 = (f32[1,2048]{1,0:T(1,128)S(1)}, f32[1,2048]{1,0:T(1,128)S(1)}, u32[]{:S(2)}, u32[]{:S(2)}) collective-permute-start(f32[1,2048]{1,0:T(1,128)S(1)} %get-tuple-element.109), channel_id=1, source_target_pairs={{0,2},{1,3},{2,4},{3,5},{4,6},{5,7},{6,0},{7,1},{8,10},{9,11},{10,... | collective-permute-start | bytes 24584 | tf_op jit(solution)/shard_map/ppermute | solution.py:24
  84.3 3.1 %backward.7 = (f32[128,2048]{1,0:T(8,128)S(1)}, bf16[128,2048]{1,0:T(8,128)(2,1)S(1)}, f32[1,2048]{1,0:T(1,128)S(1)}, f32[1,2048]{1,0:T(1,128)S(1)}) custom-call(bf16[2048,2048]{1,0:T(8,128)(2,1)S(1)} %transposed.2.refs_0_, bf16[2048,2048]{1,0:T(8,128)(2,1)S(1)} %transposed.3.refs_1_, bf16[64,2048]{1,0:T(8,128)(2,1)S(1)} %collective-permute-done.20.refs_2_.refs_10_, ...), custom_call_target="tpu_custom_call" | custom-call | flops 2147483648 | bytes 21528576 | tf_op jit(solution)/shard_map/backward/pallas_call | solution.py:42
  87.5 0.7 collective-permute-done.22.refs_2_.refs_12_
  88.2 0.4 collective-permute-done.26
  88.6 0.1 collective-permute-start.32
  88.7 0.5 collective-permute-start.31
  89.2 1.1 collective-permute-start.30
  90.3 1.7 %collective-permute-start.29 = (bf16[64,2048]{1,0:T(8,128)(2,1)S(1)}, bf16[64,2048]{1,0:T(8,128)(2,1)S(1)}, u32[]{:S(2)}, u32[]{:S(2)}) collective-permute-start(bf16[64,2048]{1,0:T(8,128)(2,1)S(1)} %collective-permute-done.22.refs_2_.refs_12_), channel_id=1, source_target_pairs={{0,24},{8,0},{16,8},{24,16},{1,25},{9,1},{17,9},{25,17},{2,26},{10... | collective-permute-start | bytes 786440 | tf_op jit(solution)/shard_map/ppermute | solution.py:29
  91.9 0.7 collective-permute-start.34
  92.7 1.1 collective-permute-start.33
  93.8 0.7 collective-permute-start.28
  94.5 3.1 %backward.8 = (f32[128,2048]{1,0:T(8,128)S(1)}, bf16[128,2048]{1,0:T(8,128)(2,1)S(1)}, f32[1,2048]{1,0:T(1,128)S(1)}, f32[1,2048]{1,0:T(1,128)S(1)}) custom-call(bf16[2048,2048]{1,0:T(8,128)(2,1)S(1)} %transposed.2.refs_0_, bf16[2048,2048]{1,0:T(8,128)(2,1)S(1)} %transposed.3.refs_1_, bf16[64,2048]{1,0:T(8,128)(2,1)S(1)} %collective-permute-done.22.refs_2_.refs_12_, ...), custom_call_target="tpu_custom_call" | custom-call | flops 2147483648 | bytes 21528576 | tf_op jit(solution)/shard_map/backward/pallas_call | solution.py:42
  97.6 1.6 %collective-permute-done.30.refs_2_ = bf16[64,2048]{1,0:T(8,128)(2,1)S(1)} collective-permute-done((bf16[64,2048]{1,0:T(8,128)(2,1)S(1)}, bf16[64,2048]{1,0:T(8,128)(2,1)S(1)}, u32[]{:S(2)}, u32[]{:S(2)}) %collective-permute-start.30) | collective-permute-done | bytes 262176 | tf_op jit(solution)/shard_map/ppermute | solution.py:24
  99.4 0.6 multiply_reduce_fusion
  100.0 1.9 %collective-permute-start.35 = (bf16[64,2048]{1,0:T(8,128)(2,1)S(1)}, bf16[64,2048]{1,0:T(8,128)(2,1)S(1)}, u32[]{:S(2)}, u32[]{:S(2)}) collective-permute-start(bf16[64,2048]{1,0:T(8,128)(2,1)S(1)} %collective-permute-done.30.refs_2_), channel_id=1, source_target_pairs={{0,24},{8,0},{16,8},{24,16},{1,25},{9,1},{17,9},{25,17},{2,26},{10... | collective-permute-start | bytes 786440 | tf_op jit(solution)/shard_map/ppermute | solution.py:29
  101.8 0.2 collective-permute-start.38
  102.1 8.1 %backward.9 = (f32[128,2048]{1,0:T(8,128)S(1)}, f32[1,2048]{1,0:T(1,128)S(1)}, f32[1,2048]{1,0:T(1,128)S(1)}, bf16[2,2048,2048]{2,1,0:T(8,128)(2,1)}) custom-call(bf16[2048,2048]{1,0:T(8,128)(2,1)S(1)} %transposed.2.refs_0_, bf16[2048,2048]{1,0:T(8,128)(2,1)S(1)} %transposed.3.refs_1_, bf16[64,2048]{1,0:T(8,128)(2,1)S(1)} %collective-permute-done.30.refs_2_, ...), custom_call_target="tpu_custom_call" | custom-call | flops 5368709120 | bytes 38830080 | tf_op jit(solution)/shard_map/backward/pallas_call | solution.py:42
  110.3 0.3 collective-permute-start.37
  110.6 1.6 %backward.10 = (bf16[128,2048]{1,0:T(8,128)(2,1)S(1)}, f32[1,2048]{1,0:T(1,128)S(1)}, f32[1,2048]{1,0:T(1,128)S(1)}) custom-call(bf16[2048,2048]{1,0:T(8,128)(2,1)S(1)} %transposed.2.refs_0_, bf16[2048,2048]{1,0:T(8,128)(2,1)S(1)} %transposed.3.refs_1_, bf16[64,2048]{1,0:T(8,128)(2,1)S(1)} %broadcast_select_fusion.1.refs_2_.refs_14_, ...), custom_call_target="tpu_custom_call" | custom-call | flops 1073741824 | bytes 19955712 | tf_op jit(solution)/shard_map/backward/pallas_call | solution.py:42
  112.2 13.8 %backward.11 = (bf16[128,2048]{1,0:T(8,128)(2,1)}, f32[1,2048]{1,0:T(1,128)}, f32[1,2048]{1,0:T(1,128)}, bf16[2,2048,2048]{2,1,0:T(8,128)(2,1)}, bf16[1,2048,2048]{2,1,0:T(8,128)(2,1)}) custom-call(bf16[2048,2048]{1,0:T(8,128)(2,1)S(1)} %transposed.2.refs_0_, bf16[2048,2048]{1,0:T(8,128)(2,1)S(1)} %transposed.3.refs_1_, ...), custom_call_target="tpu_custom_call", output_to_operand_aliasing={{3}: (29, {})} | custom-call | flops 9663676416 | bytes 69238784 | tf_op jit(solution)/shard_map/backward/pallas_call | solution.py:42
  (62 shorter events, 0.8 us)
Async XLA Ops:
  0.6 3.2 %collective-permute-start = (bf16[64,2048]{1,0:T(8,128)(2,1)}, bf16[64,2048]{1,0:T(8,128)(2,1)S(1)}, u32[]{:S(2)}, u32[]{:S(2)}) collective-permute-start(bf16[64,2048]{1,0:T(8,128)(2,1)} %bitcast.10), channel_id=1, source_target_pairs={{0,1},{1,0},{2,3},{3,2},{4,5},{5,4},{6,7},{7,6},{8,9},{9,8},{10,11... | collective-permute-start | bytes 786440 | tf_op jit(solution)/shard_map/ppermute | solution.py:19
  1.2 11.8 %collective-permute-start.1 = (bf16[64,2048]{1,0:T(8,128)(2,1)}, bf16[64,2048]{1,0:T(8,128)(2,1)S(1)}, u32[]{:S(2)}, u32[]{:S(2)}) collective-permute-start(bf16[64,2048]{1,0:T(8,128)(2,1)} %bitcast.11), channel_id=1, source_target_pairs={{0,2},{1,3},{2,4},{3,5},{4,6},{5,7},{6,0},{7,1},{8,10},{9,11},{10,... | collective-permute-start | bytes 786440 | tf_op jit(solution)/shard_map/ppermute | solution.py:24
  3.8 10.7 %copy-start.2 = (f32[1,2048]{1,0:T(1,128)S(1)}, f32[1,2048]{1,0:T(1,128)}, u32[]{:S(2)}) copy-start(f32[1,2048]{1,0:T(1,128)} %bias_ref.7) | copy-start | bytes 24580
  12.1 25.5 %copy-start = (bf16[2048,2048]{1,0:T(8,128)(2,1)}, bf16[2048,2048]{1,0:T(8,128)(2,1)S(1)}, u32[]{:S(2)}) copy-start(bf16[2048,2048]{1,0:T(8,128)(2,1)S(1)} %get-tuple-element.106.refs_1_.weight_ref) | copy-start | bytes 25165828
  12.9 1.5 %collective-permute-start.2 = (bf16[64,2048]{1,0:T(8,128)(2,1)S(1)}, bf16[64,2048]{1,0:T(8,128)(2,1)S(1)}, u32[]{:S(2)}, u32[]{:S(2)}) collective-permute-start(bf16[64,2048]{1,0:T(8,128)(2,1)S(1)} %collective-permute-done.1.mine_ref.refs_18_), channel_id=1, source_target_pairs={{0,1},{1,0},{2,3},{3,2},{4,5},{5,4},{6,7},{7,6},{8,9},{9,8},{10,11... | collective-permute-start | bytes 786440 | tf_op jit(solution)/shard_map/ppermute | solution.py:19
  13.0 10.5 %collective-permute-start.3 = (bf16[64,2048]{1,0:T(8,128)(2,1)S(1)}, bf16[64,2048]{1,0:T(8,128)(2,1)S(1)}, u32[]{:S(2)}, u32[]{:S(2)}) collective-permute-start(bf16[64,2048]{1,0:T(8,128)(2,1)S(1)} %collective-permute-done.1.mine_ref.refs_18_), channel_id=1, source_target_pairs={{0,2},{1,3},{2,4},{3,5},{4,6},{5,7},{6,0},{7,1},{8,10},{9,11},{10,... | collective-permute-start | bytes 786440 | tf_op jit(solution)/shard_map/ppermute | solution.py:24
  23.5 1.9 %collective-permute-start.4 = (bf16[64,4096]{1,0:T(8,128)(2,1)S(1)}, bf16[64,4096]{1,0:T(8,128)(2,1)S(1)}, u32[]{:S(2)}, u32[]{:S(2)}) collective-permute-start(bf16[64,4096]{1,0:T(8,128)(2,1)S(1)} %get-tuple-element.92), channel_id=1, source_target_pairs={{0,1},{1,0},{2,3},{3,2},{4,5},{5,4},{6,7},{7,6},{8,9},{9,8},{10,11... | collective-permute-start | bytes 1572872 | tf_op jit(solution)/shard_map/ppermute | solution.py:19
  23.5 10.5 %collective-permute-start.8 = (bf16[64,2048]{1,0:T(8,128)(2,1)S(1)}, bf16[64,2048]{1,0:T(8,128)(2,1)S(1)}, u32[]{:S(2)}, u32[]{:S(2)}) collective-permute-start(bf16[64,2048]{1,0:T(8,128)(2,1)S(1)} %collective-permute-done.3.mine_ref.refs_20_), channel_id=1, source_target_pairs={{0,2},{1,3},{2,4},{3,5},{4,6},{5,7},{6,0},{7,1},{8,10},{9,11},{10,... | collective-permute-start | bytes 786440 | tf_op jit(solution)/shard_map/ppermute | solution.py:24
  23.5 3.6 %collective-permute-start.7 = (bf16[64,2048]{1,0:T(8,128)(2,1)S(1)}, bf16[64,2048]{1,0:T(8,128)(2,1)S(1)}, u32[]{:S(2)}, u32[]{:S(2)}) collective-permute-start(bf16[64,2048]{1,0:T(8,128)(2,1)S(1)} %collective-permute-done.3.mine_ref.refs_20_), channel_id=1, source_target_pairs={{0,1},{1,0},{2,3},{3,2},{4,5},{5,4},{6,7},{7,6},{8,9},{9,8},{10,11... | collective-permute-start | bytes 786440 | tf_op jit(solution)/shard_map/ppermute | solution.py:19
  25.5 9.3 %collective-permute-start.5 = (bf16[64,2048]{1,0:T(8,128)(2,1)S(1)}, bf16[64,2048]{1,0:T(8,128)(2,1)S(1)}, u32[]{:S(2)}, u32[]{:S(2)}) collective-permute-start(bf16[64,2048]{1,0:T(8,128)(2,1)S(1)} %slice.67), channel_id=1, source_target_pairs={{0,8},{8,16},{16,24},{24,0},{1,9},{9,17},{17,25},{25,1},{2,10},{10... | collective-permute-start | bytes 786440 | tf_op jit(solution)/shard_map/ppermute | solution.py:29
  34.0 1.9 %collective-permute-start.9 = (bf16[64,4096]{1,0:T(8,128)(2,1)S(1)}, bf16[64,4096]{1,0:T(8,128)(2,1)S(1)}, u32[]{:S(2)}, u32[]{:S(2)}) collective-permute-start(bf16[64,4096]{1,0:T(8,128)(2,1)S(1)} %get-tuple-element.98), channel_id=1, source_target_pairs={{0,1},{1,0},{2,3},{3,2},{4,5},{5,4},{6,7},{7,6},{8,9},{9,8},{10,11... | collective-permute-start | bytes 1572872 | tf_op jit(solution)/shard_map/ppermute | solution.py:19
  34.0 3.6 %collective-permute-start.12 = (bf16[64,2048]{1,0:T(8,128)(2,1)S(1)}, bf16[64,2048]{1,0:T(8,128)(2,1)S(1)}, u32[]{:S(2)}, u32[]{:S(2)}) collective-permute-start(bf16[64,2048]{1,0:T(8,128)(2,1)S(1)} %collective-permute-done.8.mine_ref.refs_22_), channel_id=1, source_target_pairs={{0,1},{1,0},{2,3},{3,2},{4,5},{5,4},{6,7},{7,6},{8,9},{9,8},{10,11... | collective-permute-start | bytes 786440 | tf_op jit(solution)/shard_map/ppermute | solution.py:19
  34.9 9.8 %collective-permute-start.6 = (bf16[64,2048]{1,0:T(8,128)(2,1)S(1)}, bf16[64,2048]{1,0:T(8,128)(2,1)S(1)}, u32[]{:S(2)}, u32[]{:S(2)}) collective-permute-start(bf16[64,2048]{1,0:T(8,128)(2,1)S(1)} %slice_add_fusion.3), channel_id=1, source_target_pairs={{0,2},{1,3},{2,4},{3,5},{4,6},{5,7},{6,0},{7,1},{8,10},{9,11},{10,... | collective-permute-start | bytes 786440 | tf_op jit(solution)/shard_map/ppermute | solution.py:24
  36.1 9.3 %collective-permute-start.10 = (bf16[64,2048]{1,0:T(8,128)(2,1)S(1)}, bf16[64,2048]{1,0:T(8,128)(2,1)S(1)}, u32[]{:S(2)}, u32[]{:S(2)}) collective-permute-start(bf16[64,2048]{1,0:T(8,128)(2,1)S(1)} %slice.66), channel_id=1, source_target_pairs={{0,8},{8,16},{16,24},{24,0},{1,9},{9,17},{17,25},{25,1},{2,10},{10... | collective-permute-start | bytes 786440 | tf_op jit(solution)/shard_map/ppermute | solution.py:29
  45.5 2.0 %collective-permute-start.13 = (bf16[64,4096]{1,0:T(8,128)(2,1)S(1)}, bf16[64,4096]{1,0:T(8,128)(2,1)S(1)}, u32[]{:S(2)}, u32[]{:S(2)}) collective-permute-start(bf16[64,4096]{1,0:T(8,128)(2,1)S(1)} %get-tuple-element.105), channel_id=1, source_target_pairs={{0,1},{1,0},{2,3},{3,2},{4,5},{5,4},{6,7},{7,6},{8,9},{9,8},{10,11... | collective-permute-start | bytes 1572872 | tf_op jit(solution)/shard_map/ppermute | solution.py:19
  45.6 10.5 %collective-permute-start.11 = (bf16[64,2048]{1,0:T(8,128)(2,1)S(1)}, bf16[64,2048]{1,0:T(8,128)(2,1)S(1)}, u32[]{:S(2)}, u32[]{:S(2)}) collective-permute-start(bf16[64,2048]{1,0:T(8,128)(2,1)S(1)} %fusion.5), channel_id=1, source_target_pairs={{0,2},{1,3},{2,4},{3,5},{4,6},{5,7},{6,0},{7,1},{8,10},{9,11},{10,... | collective-permute-start | bytes 786440 | tf_op jit(solution)/shard_map/ppermute | solution.py:24
  47.6 9.8 %slice-start = ((s8[8388608]{0:T(1024)(128)(4,1)}), s8[4194304]{0:T(1024)(128)(4,1)S(1)}, s32[]{:S(2)}) async-start(s8[8388608]{0:T(1024)(128)(4,1)} %bitcast.8), calls=%async_computation | async-start | bytes 8388608
  47.6 9.8 %slice-start.1 = ((s8[8388608]{0:T(1024)(128)(4,1)}), s8[4194304]{0:T(1024)(128)(4,1)S(1)}, s32[]{:S(2)}) async-start(s8[8388608]{0:T(1024)(128)(4,1)} %bitcast.8), calls=%async_computation.1 | async-start | bytes 8388608
  47.6 9.3 %collective-permute-start.14 = (bf16[64,2048]{1,0:T(8,128)(2,1)S(1)}, bf16[64,2048]{1,0:T(8,128)(2,1)S(1)}, u32[]{:S(2)}, u32[]{:S(2)}) collective-permute-start(bf16[64,2048]{1,0:T(8,128)(2,1)S(1)} %slice.65), channel_id=1, source_target_pairs={{0,8},{8,16},{16,24},{24,0},{1,9},{9,17},{17,25},{25,1},{2,10},{10... | collective-permute-start | bytes 786440 | tf_op jit(solution)/shard_map/ppermute | solution.py:29
  48.5 8.6 %collective-permute-start.16 = (bf16[64,4096]{1,0:T(8,128)(2,1)S(1)}, bf16[64,4096]{1,0:T(8,128)(2,1)S(1)}, u32[]{:S(2)}, u32[]{:S(2)}) collective-permute-start(bf16[64,4096]{1,0:T(8,128)(2,1)S(1)} %get-tuple-element.91), channel_id=1, source_target_pairs={{0,1},{1,0},{2,3},{3,2},{4,5},{5,4},{6,7},{7,6},{8,9},{9,8},{10,11... | collective-permute-start | bytes 1572872 | tf_op jit(solution)/shard_map/ppermute | solution.py:19
  57.1 9.4 %collective-permute-start.15 = (bf16[64,2048]{1,0:T(8,128)(2,1)S(1)}, bf16[64,2048]{1,0:T(8,128)(2,1)S(1)}, u32[]{:S(2)}, u32[]{:S(2)}) collective-permute-start(bf16[64,2048]{1,0:T(8,128)(2,1)S(1)} %fusion.4), channel_id=1, source_target_pairs={{0,2},{1,3},{2,4},{3,5},{4,6},{5,7},{6,0},{7,1},{8,10},{9,11},{10,... | collective-permute-start | bytes 786440 | tf_op jit(solution)/shard_map/ppermute | solution.py:24
  57.3 9.2 %copy-start.3 = (bf16[1,64,2048]{2,1,0:T(8,128)(2,1)S(1)}, bf16[1,64,2048]{2,1,0:T(8,128)(2,1)}, u32[]{:S(2)}) copy-start(bf16[1,64,2048]{2,1,0:T(8,128)(2,1)} %param.7) | copy-start | bytes 786436
  57.3 9.2 %copy-start.4 = (f32[1,2048]{1,0:T(1,128)S(1)}, f32[1,2048]{1,0:T(1,128)}, u32[]{:S(2)}) copy-start(f32[1,2048]{1,0:T(1,128)} %param.11) | copy-start | bytes 24580
  57.3 9.1 %collective-permute-start.17 = (bf16[64,2048]{1,0:T(8,128)(2,1)S(1)}, bf16[64,2048]{1,0:T(8,128)(2,1)S(1)}, u32[]{:S(2)}, u32[]{:S(2)}) collective-permute-start(bf16[64,2048]{1,0:T(8,128)(2,1)S(1)} %slice.64), channel_id=1, source_target_pairs={{0,8},{8,16},{16,24},{24,0},{1,9},{9,17},{17,25},{25,1},{2,10},{10... | collective-permute-start | bytes 786440 | tf_op jit(solution)/shard_map/ppermute | solution.py:29
  66.6 1.7 %collective-permute-start.18 = (bf16[64,2048]{1,0:T(8,128)(2,1)S(1)}, bf16[64,2048]{1,0:T(8,128)(2,1)S(1)}, u32[]{:S(2)}, u32[]{:S(2)}) collective-permute-start(bf16[64,2048]{1,0:T(8,128)(2,1)S(1)} %fusion.3.refs_2_.refs_8_), channel_id=1, source_target_pairs={{0,1},{1,0},{2,3},{3,2},{4,5},{5,4},{6,7},{7,6},{8,9},{9,8},{10,11... | collective-permute-start | bytes 786440 | tf_op jit(solution)/shard_map/ppermute | solution.py:19
  66.7 10.5 %collective-permute-start.20 = (bf16[64,2048]{1,0:T(8,128)(2,1)S(1)}, bf16[64,2048]{1,0:T(8,128)(2,1)S(1)}, u32[]{:S(2)}, u32[]{:S(2)}) collective-permute-start(bf16[64,2048]{1,0:T(8,128)(2,1)S(1)} %fusion.3.refs_2_.refs_8_), channel_id=1, source_target_pairs={{0,2},{1,3},{2,4},{3,5},{4,6},{5,7},{6,0},{7,1},{8,10},{9,11},{10,... | collective-permute-start | bytes 786440 | tf_op jit(solution)/shard_map/ppermute | solution.py:24
  67.3 9.9 %collective-permute-start.24 = (bf16[64,2048]{1,0:T(8,128)(2,1)S(1)}, bf16[64,2048]{1,0:T(8,128)(2,1)S(1)}, u32[]{:S(2)}, u32[]{:S(2)}) collective-permute-start(bf16[64,2048]{1,0:T(8,128)(2,1)S(1)} %fusion.3.refs_2_.refs_8_), channel_id=1, source_target_pairs={{0,24},{8,0},{16,8},{24,16},{1,25},{9,1},{17,9},{25,17},{2,26},{10... | collective-permute-start | bytes 786440 | tf_op jit(solution)/shard_map/ppermute | solution.py:29
  77.2 5.7 %collective-permute-start.25 = (bf16[64,2048]{1,0:T(8,128)(2,1)S(1)}, bf16[64,2048]{1,0:T(8,128)(2,1)S(1)}, u32[]{:S(2)}, u32[]{:S(2)}) collective-permute-start(bf16[64,2048]{1,0:T(8,128)(2,1)S(1)} %broadcast_select_fusion.3.refs_4_.refs_10_), channel_id=1, source_target_pairs={{0,1},{1,0},{2,3},{3,2},{4,5},{5,4},{6,7},{7,6},{8,9},{9,8},{10,11... | collective-permute-start | bytes 786440 | tf_op jit(solution)/shard_map/ppermute | solution.py:19
  77.3 5.6 %collective-permute-start.23 = (bf16[64,2048]{1,0:T(8,128)(2,1)S(1)}, bf16[64,2048]{1,0:T(8,128)(2,1)S(1)}, u32[]{:S(2)}, u32[]{:S(2)}) collective-permute-start(bf16[64,2048]{1,0:T(8,128)(2,1)S(1)} %collective-permute-done.20.refs_2_.refs_10_), channel_id=1, source_target_pairs={{0,1},{1,0},{2,3},{3,2},{4,5},{5,4},{6,7},{7,6},{8,9},{9,8},{10,11... | collective-permute-start | bytes 786440 | tf_op jit(solution)/shard_map/ppermute | solution.py:19
  77.8 10.4 %collective-permute-start.22 = (bf16[64,2048]{1,0:T(8,128)(2,1)S(1)}, bf16[64,2048]{1,0:T(8,128)(2,1)S(1)}, u32[]{:S(2)}, u32[]{:S(2)}) collective-permute-start(bf16[64,2048]{1,0:T(8,128)(2,1)S(1)} %collective-permute-done.20.refs_2_.refs_10_), channel_id=1, source_target_pairs={{0,2},{1,3},{2,4},{3,5},{4,6},{5,7},{6,0},{7,1},{8,10},{9,11},{10,... | collective-permute-start | bytes 786440 | tf_op jit(solution)/shard_map/ppermute | solution.py:24
  78.1 10.1 %collective-permute-start.21 = (bf16[64,2048]{1,0:T(8,128)(2,1)S(1)}, bf16[64,2048]{1,0:T(8,128)(2,1)S(1)}, u32[]{:S(2)}, u32[]{:S(2)}) collective-permute-start(bf16[64,2048]{1,0:T(8,128)(2,1)S(1)} %collective-permute-done.20.refs_2_.refs_10_), channel_id=1, source_target_pairs={{0,24},{8,0},{16,8},{24,16},{1,25},{9,1},{17,9},{25,17},{2,26},{10... | collective-permute-start | bytes 786440 | tf_op jit(solution)/shard_map/ppermute | solution.py:29
  79.4 8.9 %collective-permute-start.27 = (f32[1,2048]{1,0:T(1,128)S(1)}, f32[1,2048]{1,0:T(1,128)S(1)}, u32[]{:S(2)}, u32[]{:S(2)}) collective-permute-start(f32[1,2048]{1,0:T(1,128)S(1)} %get-tuple-element.109), channel_id=1, source_target_pairs={{0,6},{1,7},{2,0},{3,1},{4,2},{5,3},{6,4},{7,5},{8,14},{9,15},{10,... | collective-permute-start | bytes 24584 | tf_op jit(solution)/shard_map/ppermute | solution.py:24
  82.9 5.7 %collective-permute-start.26 = (f32[1,2048]{1,0:T(1,128)S(1)}, f32[1,2048]{1,0:T(1,128)S(1)}, u32[]{:S(2)}, u32[]{:S(2)}) collective-permute-start(f32[1,2048]{1,0:T(1,128)S(1)} %get-tuple-element.109), channel_id=1, source_target_pairs={{0,4},{1,5},{2,6},{3,7},{4,0},{5,1},{6,2},{7,3},{8,12},{9,13},{10,... | collective-permute-start | bytes 24584 | tf_op jit(solution)/shard_map/ppermute | solution.py:24
  82.9 5.7 %collective-permute-start.19 = (f32[1,2048]{1,0:T(1,128)S(1)}, f32[1,2048]{1,0:T(1,128)S(1)}, u32[]{:S(2)}, u32[]{:S(2)}) collective-permute-start(f32[1,2048]{1,0:T(1,128)S(1)} %get-tuple-element.109), channel_id=1, source_target_pairs={{0,2},{1,3},{2,4},{3,5},{4,6},{5,7},{6,0},{7,1},{8,10},{9,11},{10,... | collective-permute-start | bytes 24584 | tf_op jit(solution)/shard_map/ppermute | solution.py:24
  88.6 4.0 %collective-permute-start.32 = (bf16[64,2048]{1,0:T(8,128)(2,1)S(1)}, bf16[64,2048]{1,0:T(8,128)(2,1)S(1)}, u32[]{:S(2)}, u32[]{:S(2)}) collective-permute-start(bf16[64,2048]{1,0:T(8,128)(2,1)S(1)} %broadcast_select_fusion.2.refs_4_.refs_12_), channel_id=1, source_target_pairs={{0,1},{1,0},{2,3},{3,2},{4,5},{5,4},{6,7},{7,6},{8,9},{9,8},{10,11... | collective-permute-start | bytes 786440 | tf_op jit(solution)/shard_map/ppermute | solution.py:19
  88.7 5.0 %collective-permute-start.31 = (bf16[64,2048]{1,0:T(8,128)(2,1)S(1)}, bf16[64,2048]{1,0:T(8,128)(2,1)S(1)}, u32[]{:S(2)}, u32[]{:S(2)}) collective-permute-start(bf16[64,2048]{1,0:T(8,128)(2,1)S(1)} %collective-permute-done.22.refs_2_.refs_12_), channel_id=1, source_target_pairs={{0,1},{1,0},{2,3},{3,2},{4,5},{5,4},{6,7},{7,6},{8,9},{9,8},{10,11... | collective-permute-start | bytes 786440 | tf_op jit(solution)/shard_map/ppermute | solution.py:19
  89.2 10.1 %collective-permute-start.30 = (bf16[64,2048]{1,0:T(8,128)(2,1)S(1)}, bf16[64,2048]{1,0:T(8,128)(2,1)S(1)}, u32[]{:S(2)}, u32[]{:S(2)}) collective-permute-start(bf16[64,2048]{1,0:T(8,128)(2,1)S(1)} %collective-permute-done.22.refs_2_.refs_12_), channel_id=1, source_target_pairs={{0,2},{1,3},{2,4},{3,5},{4,6},{5,7},{6,0},{7,1},{8,10},{9,11},{10,... | collective-permute-start | bytes 786440 | tf_op jit(solution)/shard_map/ppermute | solution.py:24
  90.3 9.0 %collective-permute-start.29 = (bf16[64,2048]{1,0:T(8,128)(2,1)S(1)}, bf16[64,2048]{1,0:T(8,128)(2,1)S(1)}, u32[]{:S(2)}, u32[]{:S(2)}) collective-permute-start(bf16[64,2048]{1,0:T(8,128)(2,1)S(1)} %collective-permute-done.22.refs_2_.refs_12_), channel_id=1, source_target_pairs={{0,24},{8,0},{16,8},{24,16},{1,25},{9,1},{17,9},{25,17},{2,26},{10... | collective-permute-start | bytes 786440 | tf_op jit(solution)/shard_map/ppermute | solution.py:29
  91.9 7.4 %collective-permute-start.34 = (f32[1,2048]{1,0:T(1,128)S(1)}, f32[1,2048]{1,0:T(1,128)S(1)}, u32[]{:S(2)}, u32[]{:S(2)}) collective-permute-start(f32[1,2048]{1,0:T(1,128)S(1)} %add_add_fusion.1), channel_id=1, source_target_pairs={{0,24},{8,0},{16,8},{24,16},{1,25},{9,1},{17,9},{25,17},{2,26},{10... | collective-permute-start | bytes 24584 | tf_op jit(solution)/shard_map/ppermute | solution.py:29
  92.7 6.7 %collective-permute-start.33 = (f32[1,2048]{1,0:T(1,128)S(1)}, f32[1,2048]{1,0:T(1,128)S(1)}, u32[]{:S(2)}, u32[]{:S(2)}) collective-permute-start(f32[1,2048]{1,0:T(1,128)S(1)} %add_add_fusion.1), channel_id=1, source_target_pairs={{0,16},{8,24},{16,0},{24,8},{1,17},{9,25},{17,1},{25,9},{2,18},{10... | collective-permute-start | bytes 24584 | tf_op jit(solution)/shard_map/ppermute | solution.py:29
  93.8 5.6 %collective-permute-start.28 = (f32[1,2048]{1,0:T(1,128)S(1)}, f32[1,2048]{1,0:T(1,128)S(1)}, u32[]{:S(2)}, u32[]{:S(2)}) collective-permute-start(f32[1,2048]{1,0:T(1,128)S(1)} %add_add_fusion.1), channel_id=1, source_target_pairs={{0,8},{8,16},{16,24},{24,0},{1,9},{9,17},{17,25},{25,1},{2,10},{10... | collective-permute-start | bytes 24584 | tf_op jit(solution)/shard_map/ppermute | solution.py:29
  100.0 2.1 %collective-permute-start.36 = (bf16[64,2048]{1,0:T(8,128)(2,1)S(1)}, bf16[64,2048]{1,0:T(8,128)(2,1)S(1)}, u32[]{:S(2)}, u32[]{:S(2)}) collective-permute-start(bf16[64,2048]{1,0:T(8,128)(2,1)S(1)} %collective-permute-done.30.refs_2_), channel_id=1, source_target_pairs={{0,1},{1,0},{2,3},{3,2},{4,5},{5,4},{6,7},{7,6},{8,9},{9,8},{10,11... | collective-permute-start | bytes 786440 | tf_op jit(solution)/shard_map/ppermute | solution.py:19
  100.0 10.2 %collective-permute-start.35 = (bf16[64,2048]{1,0:T(8,128)(2,1)S(1)}, bf16[64,2048]{1,0:T(8,128)(2,1)S(1)}, u32[]{:S(2)}, u32[]{:S(2)}) collective-permute-start(bf16[64,2048]{1,0:T(8,128)(2,1)S(1)} %collective-permute-done.30.refs_2_), channel_id=1, source_target_pairs={{0,24},{8,0},{16,8},{24,16},{1,25},{9,1},{17,9},{25,17},{2,26},{10... | collective-permute-start | bytes 786440 | tf_op jit(solution)/shard_map/ppermute | solution.py:29
  101.8 8.8 %collective-permute-start.38 = (bf16[64,2048]{1,0:T(8,128)(2,1)S(1)}, bf16[64,2048]{1,0:T(8,128)(2,1)S(1)}, u32[]{:S(2)}, u32[]{:S(2)}) collective-permute-start(bf16[64,2048]{1,0:T(8,128)(2,1)S(1)} %broadcast_select_fusion.1.refs_2_.refs_14_), channel_id=1, source_target_pairs={{0,1},{1,0},{2,3},{3,2},{4,5},{5,4},{6,7},{7,6},{8,9},{9,8},{10,11... | collective-permute-start | bytes 786440 | tf_op jit(solution)/shard_map/ppermute | solution.py:19
  110.3 1.9 %collective-permute-start.37 = (bf16[64,2048]{1,0:T(8,128)(2,1)S(1)}, bf16[64,2048]{1,0:T(8,128)(2,1)S(1)}, u32[]{:S(2)}, u32[]{:S(2)}) collective-permute-start(bf16[64,2048]{1,0:T(8,128)(2,1)S(1)} %broadcast_select_fusion.refs_2_), channel_id=1, source_target_pairs={{0,1},{1,0},{2,3},{3,2},{4,5},{5,4},{6,7},{7,6},{8,9},{9,8},{10,11... | collective-permute-start | bytes 786440 | tf_op jit(solution)/shard_map/ppermute | solution.py:19
  110.6 1.6 %copy-start.1 = (bf16[1,64,2048]{2,1,0:T(8,128)(2,1)S(1)}, bf16[1,64,2048]{2,1,0:T(8,128)(2,1)}, u32[]{:S(2)}) copy-start(bf16[1,64,2048]{2,1,0:T(8,128)(2,1)} %param.6) | copy-start | bytes 786436
